TPU v7x, 256 devices: a whole 4x4x8 slice. The times are simulated.
256 devices in a mesh: inner: 16 (over x_hi, z), outer: 16 (over y, x_lo, core).
Axes of the slice: x: 4 (x_hi: 2, x_lo: 2; x = x_hi * 2 + x_lo), y: 4, z: 8, core: 2. Of those that a mesh axis runs over, the one named last changes fastest.
Arguments:
- queries: bfloat16 [65536, 768], P(('outer', 'inner')), may hold values from -24 to 24
- keys: bfloat16 [65536, 768], P(('outer', 'inner')), may hold values from -24 to 24
- values: bfloat16 [65536, 768], P(('outer', 'inner')), may hold values from -6 to 6
- saved_out: bfloat16 [65536, 768], P(('outer', 'inner')), may hold values from -6 to 6
- out_grad: bfloat16 [65536, 768], P(('outer', 'inner')), may hold values from -192 to 192
- offset_mid: int32 [12], replicated, may hold values from 0 to 3
- offset_wide: int32 [12], replicated, may hold values from 0 to 63
Outputs:
- query_grads: bfloat16 [65536, 768], P(('outer', 'inner'))
- key_grads: bfloat16 [65536, 768], P(('outer', 'inner'))
- value_grads: bfloat16 [65536, 768], P(('outer', 'inner'))
All inputs are finite; a program needn't handle non-finite values.
Results may differ from a plain program's by a relative error of at most 0.0049.
Values may be sent and summed in bfloat16 or wider, within the bound.
A program may use at most 128 MiB of HBM per device.

v0:
```python
import math

import jax
import jax.numpy as jnp
from jax import lax
from jax.sharding import PartitionSpec as P

RATE_MID = 4
RATE_WIDE = 64


def select_rows(block, offsets, rate):
    shape = block.shape
    split = block.reshape(shape[:-3] + (shape[-3] // rate, rate) + shape[-2:])
    chosen = jnp.arange(rate, dtype=jnp.int32)[:, None] == offsets[None, :]
    return jnp.sum(jnp.where(chosen[:, :, None], split, jnp.zeros((), block.dtype)), axis=-3)


def spread_rows(picked, offsets, rate):
    shape = picked.shape
    chosen = jnp.arange(rate, dtype=jnp.int32)[:, None] == offsets[None, :]
    full = jnp.where(chosen[:, :, None], jnp.expand_dims(picked, -3), jnp.zeros((), picked.dtype))
    return full.reshape(shape[:-3] + (shape[-3] * rate,) + shape[-2:])


def branch_lse(queries, keys, scaling_multiplier):
    logit_scores = (
        jnp.einsum("rpj,xpj->prx", queries, keys, preferred_element_type=jnp.float32)
        * scaling_multiplier
    )
    highest = jnp.max(logit_scores, axis=-1, keepdims=True)
    return jnp.transpose(
        highest[..., 0] + jnp.log(jnp.sum(jnp.exp(logit_scores - highest), axis=-1))
    )


def branch_grads(queries, output_gradient, lse, deltas, keys, values, scaling_multiplier):
    logit_scores = (
        jnp.einsum("rpj,xpj->prx", queries, keys, preferred_element_type=jnp.float32)
        * scaling_multiplier
    )
    probs = jnp.exp(logit_scores - jnp.transpose(lse)[:, :, None])
    attention_weights = probs.astype(jnp.bfloat16)
    value_segment_slice = jnp.einsum(
        "vsy,svo->yvo", attention_weights, output_gradient, preferred_element_type=jnp.float32
    )
    probability_gradient = jnp.einsum(
        "rpj,xpj->prx", output_gradient, values, preferred_element_type=jnp.float32
    )
    score_gradient = (probs * (probability_gradient - jnp.transpose(deltas)[:, :, None])).astype(
        jnp.bfloat16
    )
    query_segment_slice = (
        jnp.einsum("szr,rsx->zsx", score_gradient, keys, preferred_element_type=jnp.float32)
        * scaling_multiplier
    )
    key_segment_slice = (
        jnp.einsum("vsy,svo->yvo", score_gradient, queries, preferred_element_type=jnp.float32)
        * scaling_multiplier
    )
    return (query_segment_slice, key_segment_slice, value_segment_slice)


def merge_lse(local, mid_full, mid_mask, wide_full, wide_mask):
    mid_value = jnp.where(mid_mask, mid_full, local)
    wide_value = jnp.where(wide_mask, wide_full, local)
    highest = jnp.maximum(local, jnp.maximum(mid_value, wide_value))
    summed = jnp.exp(local - highest)
    summed = summed + jnp.where(mid_mask, jnp.exp(mid_value - highest), 0.0)
    summed = summed + jnp.where(wide_mask, jnp.exp(wide_value - highest), 0.0)
    return highest + jnp.log(summed)


def per_device(queries, keys, values, saved_out, out_grad, offset_mid, offset_wide):
    tok_count = queries.shape[0]
    model_width = queries.shape[1]
    head_count = offset_mid.shape[0]
    head_dim = model_width // head_count
    scaling_multiplier = 1.0 / math.sqrt(head_dim)
    unpacked = (tok_count, head_count, head_dim)

    def flatten(block):
        return block.reshape(block.shape[0], model_width)

    def to_heads(block):
        return block.reshape(block.shape[0], head_count, head_dim)

    query_rows = queries.reshape(unpacked)
    key_rows = keys.reshape(unpacked)
    value_rows = values.reshape(unpacked)
    grad_rows = out_grad.reshape(unpacked)
    deltas = jnp.sum(
        grad_rows.astype(jnp.float32) * saved_out.reshape(unpacked).astype(jnp.float32), axis=-1
    )
    query_mid, key_mid, value_mid, grad_mid = [
        select_rows(block, offset_mid, RATE_MID)
        for block in (query_rows, key_rows, value_rows, grad_rows)
    ]
    query_wide, key_wide, value_wide, grad_wide = [
        select_rows(block, offset_wide, RATE_WIDE)
        for block in (query_rows, key_rows, value_rows, grad_rows)
    ]
    mid_keys, mid_values = (
        lax.all_gather(flatten(key_mid), "inner", axis=0, tiled=True),
        lax.all_gather(flatten(value_mid), "inner", axis=0, tiled=True),
    )
    wide_keys, wide_values = (
        lax.all_gather(flatten(key_wide), ("outer", "inner"), axis=0, tiled=True),
        lax.all_gather(flatten(value_wide), ("outer", "inner"), axis=0, tiled=True),
    )
    mid_keys = to_heads(mid_keys)
    mid_values = to_heads(mid_values)
    wide_keys = to_heads(wide_keys)
    wide_values = to_heads(wide_values)
    lse_local = branch_lse(query_rows, key_rows, scaling_multiplier)
    lse_mid = branch_lse(query_mid, mid_keys, scaling_multiplier)
    lse_wide = branch_lse(query_wide, wide_keys, scaling_multiplier)
    position = jnp.arange(tok_count, dtype=jnp.int32)
    mid_mask = (position % RATE_MID)[:, None] == offset_mid[None, :]
    wide_mask = (position % RATE_WIDE)[:, None] == offset_wide[None, :]
    mid_full = spread_rows(lse_mid[..., None], offset_mid, RATE_MID)[..., 0]
    wide_full = spread_rows(lse_wide[..., None], offset_wide, RATE_WIDE)[..., 0]
    lse_total = merge_lse(lse_local, mid_full, mid_mask, wide_full, wide_mask)
    lse_mid_rows = select_rows(lse_total[..., None], offset_mid, RATE_MID)[..., 0]
    delta_mid_rows = select_rows(deltas[..., None], offset_mid, RATE_MID)[..., 0]
    lse_wide_rows = select_rows(lse_total[..., None], offset_wide, RATE_WIDE)[..., 0]
    delta_wide_rows = select_rows(deltas[..., None], offset_wide, RATE_WIDE)[..., 0]
    grad_q_local, grad_k_local, grad_v_local = branch_grads(
        query_rows, grad_rows, lse_total, deltas, key_rows, value_rows, scaling_multiplier
    )
    grad_q_mid, mid_key_terms, mid_value_terms = branch_grads(
        query_mid, grad_mid, lse_mid_rows, delta_mid_rows, mid_keys, mid_values, scaling_multiplier
    )
    grad_k_mid, grad_v_mid = (
        lax.psum_scatter(flatten(mid_key_terms), "inner", scatter_dimension=0, tiled=True),
        lax.psum_scatter(flatten(mid_value_terms), "inner", scatter_dimension=0, tiled=True),
    )
    grad_k_mid = to_heads(grad_k_mid)
    grad_v_mid = to_heads(grad_v_mid)
    grad_q_wide, wide_key_terms, wide_value_terms = branch_grads(
        query_wide,
        grad_wide,
        lse_wide_rows,
        delta_wide_rows,
        wide_keys,
        wide_values,
        scaling_multiplier,
    )
    grad_k_wide, grad_v_wide = (
        lax.psum_scatter(
            flatten(wide_key_terms), ("outer", "inner"), scatter_dimension=0, tiled=True
        ),
        lax.psum_scatter(
            flatten(wide_value_terms), ("outer", "inner"), scatter_dimension=0, tiled=True
        ),
    )
    grad_k_wide = to_heads(grad_k_wide)
    grad_v_wide = to_heads(grad_v_wide)

    def combine(local_part, mid_part, wide_part):
        summed = (
            local_part
            + spread_rows(mid_part, offset_mid, RATE_MID)
            + spread_rows(wide_part, offset_wide, RATE_WIDE)
        )
        return summed.astype(jnp.bfloat16).reshape(tok_count, model_width)

    query_grads = combine(grad_q_local, grad_q_mid, grad_q_wide)
    key_grads = combine(grad_k_local, grad_k_mid, grad_k_wide)
    value_grads = combine(grad_v_local, grad_v_mid, grad_v_wide)
    return (query_grads, key_grads, value_grads)


def solution(mesh):
    in_specs = (
        P(("outer", "inner"), None),
        P(("outer", "inner"), None),
        P(("outer", "inner"), None),
        P(("outer", "inner"), None),
        P(("outer", "inner"), None),
        P(),
        P(),
    )
    out_specs = (
        P(("outer", "inner"), None),
        P(("outer", "inner"), None),
        P(("outer", "inner"), None),
    )
    return jax.shard_map(
        per_device, mesh=mesh, in_specs=in_specs, out_specs=out_specs, check_vma=False
    )
```

profile of v0, /device:TPU:1, one launch (start us, length us, event | category | flops | bytes accessed | tf_op | source)
XLA Modules:
  0.0 2289.8 jit_solution(5871275884735236147)
XLA Ops:
  11.9 2.5 reshape_reshape.28
  14.3 4.1 select_reduce_fusion
  27.6 5.7 select_reduce_fusion.4
  47.8 55.1 %all-gather.7.cloned.1.call-done = bf16[1024,768]{1,0:T(8,128)(2,1)} async-done(((bf16[64,768]{1,0:T(8,128)(2,1)}), bf16[1024,768]{1,0:T(8,128)(2,1)}) %all-gather.7.cloned.1.call-update) | async-done | bytes 1572880 | tf_op jit(solution)/shard_map/all_gather | solution.py:104
  102.9 2.6 copy.121
  105.4 2.2 multiply_reduce_fusion
  112.1 681.1 %all-gather.11.cloned.1.call-done = bf16[256,4,768]{2,1,0:T(4,128)(2,1)} async-done(((bf16[1,4,768]{2,1,0:T(4,128)(2,1)}), bf16[256,4,768]{2,1,0:T(4,128)(2,1)}) %all-gather.11.cloned.1.call-update) | async-done | bytes 1572880 | tf_op jit(solution)/shard_map/all_gather | solution.py:108
  793.2 6.0 reshape.192
  799.2 5.3 copy.130
  804.5 2.0 fusion.55
  815.4 666.9 %all-gather.13.cloned.1.call-done = bf16[256,4,768]{2,1,0:T(4,128)(2,1)} async-done(((bf16[1,4,768]{2,1,0:T(4,128)(2,1)}), bf16[256,4,768]{2,1,0:T(4,128)(2,1)}) %all-gather.13.cloned.1.call-update) | async-done | bytes 1572880 | tf_op jit(solution)/shard_map/all_gather | solution.py:109
  1482.3 6.1 reshape.198
  1488.4 4.0 fusion.39
  1492.5 2.2 convolution_multiply_fusion.1
  1494.7 2.3 fusion.45
  1502.1 3.4 fusion.4
  1505.5 3.5 copy.186
  1509.3 53.3 %all-gather.9.cloned.1.call-done = bf16[1024,768]{1,0:T(8,128)(2,1)} async-done(((bf16[64,768]{1,0:T(8,128)(2,1)}), bf16[1024,768]{1,0:T(8,128)(2,1)}) %all-gather.9.cloned.1.call-update) | async-done | bytes 1572880 | tf_op jit(solution)/shard_map/all_gather | solution.py:105
  1562.6 2.6 copy.139
  1566.7 2.5 multiply_convert_fusion
  1571.0 2.5 copy.182
  1576.9 1.9 copy.143
  1578.8 2.1 fusion.42
  1581.1 1.9 broadcast_in_dim.300
  1583.0 3.2 broadcast_in_dim.301
  1586.2 2.5 broadcast_in_dim.294
  1588.6 2.8 copy.144
  1591.4 2.0 multiply_convert_fusion.1
  1595.8 1.9 copy.167
  1597.7 243.8 %all-reduce.5.cloned.1.call-done = (f32[1024,768]{0,1:T(8,128)}, f32[1024,768]{0,1:T(8,128)}) async-done(((f32[1024,768]{0,1:T(8,128)}, f32[1024,768]{0,1:T(8,128)}), (f32[1024,768]{0,1:T(8,128)}, f32[1024,768]{0,1:T(8,128)})) %all-reduce.5.cloned.1.call-update) | async-done | bytes 6291472
  1842.7 1.9 broadcast_in_dim.306
  1844.5 3.0 broadcast_in_dim.307
  1848.7 1.9 broadcast_in_dim.312
  1850.5 3.0 broadcast_in_dim.313
  1853.5 198.6 %reduce-scatter.11.cloned.1.call-done = f32[64,768]{1,0:T(8,128)} async-done(((f32[1024,768]{1,0:T(8,128)}), f32[64,768]{1,0:T(8,128)}) %reduce-scatter.11.cloned.1.call-update) | async-done | bytes 196624
  2052.1 1.8 copy.187
  2053.9 1.9 copy.164
  2055.8 2.5 broadcast_in_dim.309
  2058.3 2.8 copy.165
  2061.0 203.0 %reduce-scatter.9.cloned.1.call-done = f32[64,768]{1,0:T(8,128)} async-done(((f32[1024,768]{1,0:T(8,128)}), f32[64,768]{1,0:T(8,128)}) %reduce-scatter.9.cloned.1.call-update) | async-done | bytes 196624
  2264.0 1.8 copy.183
  2265.9 1.9 copy.159
  2267.8 2.5 broadcast_in_dim.303
  2270.2 2.7 copy.160
  2273.0 3.3 fusion.31
  2276.3 1.9 copy.168
  2278.2 2.8 fusion.27
  2281.0 1.9 copy.169
  (124 shorter events, 57.6 us)
Async XLA Ops:
  7.2 4.1 copy-start.18
  7.2 95.7 %all-gather.7.cloned.1.call-start = ((), (), s32[]{:S(2)}) async-start(), calls=%async_computation.2 | async-start | bytes 1671168 | tf_op jit(solution)/shard_map/all_gather | solution.py:104
  7.9 32.7 %copy-start.26 = (pred[4,12]{1,0:T(4,128)(4,1)}, pred[4,12]{1,0:T(4,128)(4,1)S(1)}, u32[]{:S(2)}) copy-start(pred[4,12]{1,0:T(4,128)(4,1)S(1)} %iota_compare_fusion.1) | copy-start | bytes 148
  14.3 5.9 copy-start.17
  20.2 772.9 %all-gather.11.cloned.1.call-start = ((), (), s32[]{:S(2)}) async-start(), calls=%async_computation.4 | async-start | bytes 1579008 | tf_op jit(solution)/shard_map/all_gather | solution.py:108
  20.4 23.9 %copy-start.6 = (bf16[256,768]{0,1:T(8,128)(2,1)}, bf16[256,768]{0,1:T(8,128)(2,1)S(1)}, u32[]{:S(2)}) copy-start(bf16[256,768]{0,1:T(8,128)(2,1)S(1)} %copy.119) | copy-start | bytes 1179652
  21.8 22.6 copy-start.7
  21.8 5.7 copy-start.27
  23.1 10.2 copy-start.9
  27.6 15.9 copy-start.19
  34.9 1447.4 %all-gather.13.cloned.1.call-start = ((), (), s32[]{:S(2)}) async-start(), calls=%async_computation.5 | async-start | bytes 1579008 | tf_op jit(solution)/shard_map/all_gather | solution.py:109
  36.7 1526.0 %all-gather.9.cloned.1.call-start = ((), (), s32[]{:S(2)}) async-start(), calls=%async_computation.3 | async-start | bytes 1671168 | tf_op jit(solution)/shard_map/all_gather | solution.py:105
  38.5 1803.0 %all-reduce.5.cloned.1.call-start = ((), (), s32[]{:S(2)}) async-start(), calls=%async_computation.8 | async-start | bytes 12582912
  42.6 5.1 copy-start.22
  45.0 1.6 copy-start
  45.0 60.4 %copy-start.21 = (f32[12,256]{1,0:T(8,128)}, f32[12,256]{1,0:T(8,128)S(1)}, u32[]{:S(2)}) copy-start(f32[12,256]{1,0:T(8,128)S(1)} %get-tuple-element.33) | copy-start | bytes 36868
  806.5 0.7 copy-start.10
  1488.4 4.1 copy-start.16
  1488.4 6.3 copy-start.11
  1488.4 6.3 copy-start.14
  1488.4 6.3 copy-start.25
  1492.5 4.5 copy-start.20
  1497.0 555.1 %reduce-scatter.11.cloned.1.call-start = ((), (), s32[]{:S(2)}) async-start(), calls=%async_computation.7 | async-start | bytes 3342336
  1509.0 755.0 %reduce-scatter.9.cloned.1.call-start = ((), (), s32[]{:S(2)}) async-start(), calls=%async_computation.6 | async-start | bytes 3342336
  1566.7 3.7 copy-start.15
  1569.3 1.1 copy-start.3
  1573.4 2.1 copy-start.2
  1573.4 2.1 copy-start.4
  1583.0 8.4 copy-start.1
  1591.4 3.3 copy-start.8
  1591.4 3.3 copy-start.12
  1591.4 3.3 copy-start.13
  1591.4 3.3 copy-start.23
  1591.4 3.3 copy-start.24
  1593.5 1.2 copy-start.5
Sparse Core Ops, SparseCore 0:
  20.3 82.4 all-gather.6
  104.7 688.3 all-gather.10
  795.0 687.2 all-gather.12
  1484.8 77.8 all-gather.8
  1568.1 273.3 all-reduce.4
  1845.9 206.1 reduce-scatter.10
  2056.1 207.8 reduce-scatter.8
where the time goes:
time: 2290 us
  waiting for transfers between devices  2100 us (92%)
  local copies, waits for them, and re-layouts  122 us (5%)
  matrix products  32.6 us (1%)
    all_gather x1, waiting for transfers between devices, per_device(): lax.all_gather(flatten(key_wide), ('outer', 'inner'), axis=0, tiled=True)  681 us
    all_gather x1, waiting for transfers between devices, per_device(): lax.all_gather(flatten(value_wide), ('outer', 'inner'), axis=0, tiled=True)  667 us
    unnamed x10, waiting for transfers between devices  645 us
    all_gather x1, waiting for transfers between devices, per_device(): lax.all_gather(flatten(key_mid), 'inner', axis=0, tiled=True)  55.1 us
    all_gather x1, waiting for transfers between devices, per_device(): lax.all_gather(flatten(value_mid), 'inner', axis=0, tiled=True)  53.3 us
  transfers between devices with their start and end apart: 7, of which 7 were waited for; matrix products, arithmetic and copies ran while one was open for 6% of the time, Pallas kernels for 0%

commit v1 on v0

v1 whole, which is shorter than its diff:
```python
import jax
import jax.numpy as jnp
from jax import lax
from jax.experimental import pallas as pl
from jax.experimental.pallas import tpu as pltpu
from jax.sharding import PartitionSpec as P

BF = jnp.bfloat16
F32 = jnp.float32
I32 = jnp.int32

N = 16
HEADS = 12
T = 256
MID = 64
SCALE = 0.125
NEG = -1e30
MSG = 144
RET = 96


def iota(shape, dim):
    return lax.broadcasted_iota(I32, shape, dim)


def nn(a, b):
    return lax.dot_general(a, b, (((1,), (0,)), ((), ())), preferred_element_type=F32)


def nt(a, b):
    return lax.dot_general(a, b, (((1,), (1,)), ((), ())), preferred_element_type=F32)


def tn(a, b):
    return lax.dot_general(a, b, (((0,), (0,)), ((), ())), preferred_element_type=F32)


def onehot(mask):
    return jnp.where(mask, 1.0, 0.0).astype(BF)


def split3(x):
    a = x.astype(BF).astype(F32)
    r = x - a
    b = r.astype(BF).astype(F32)
    return jnp.concatenate([a, b, r - b], axis=0).astype(BF)


def sum3(x):
    r = x.shape[0] // 3
    return x[:r] + x[r : 2 * r] + x[2 * r :]


def lse3(a, b, c):
    top = jnp.maximum(a, jnp.maximum(b, c))
    return top + jnp.log(jnp.exp(a - top) + jnp.exp(b - top) + jnp.exp(c - top))


def swap(x):
    return pltpu.roll(x, 64, 1)


def device_of(h):
    return (h // 3) * 4 + h % 3


def kernel(
    om_ref, ow_ref, q_ref, k_ref, v_ref, o_ref, g_ref,
    dq_ref, dk_ref, dv_ref,
    xl, yl, msg, rx, el, gl, mst, st_tx, st_rx, ls_tx, ls_rx,
    yk, yv, s_scr, em, gm, mm, ml, dm, xw_all, xw_w, yw, rxo, wp, rxp,
    ret, retw, ret_rx, retw_rx, acc_kv, acc_q,
    msg_s, msg_r, st_s, st_r, ls_s, ls_r, yw_s, yw_r, wp_s, wp_r, ret_s, ret_r, retw_s, retw_r,
):
    inner = lax.axis_index("inner")
    outer = lax.axis_index("outer")
    active = inner % 4 < 3
    head = jnp.minimum((inner // 4) * 3 + inner % 4, HEADS - 1)

    def to_inner(src, dst, send, recv, target):
        return pltpu.make_async_remote_copy(
            src_ref=src, dst_ref=dst, send_sem=send, recv_sem=recv,
            device_id={"inner": target}, device_id_type=pl.DeviceIdType.MESH,
        )

    def to_outer(src, dst, send, recv, target):
        return pltpu.make_async_remote_copy(
            src_ref=src, dst_ref=dst, send_sem=send, recv_sem=recv,
            device_id={"outer": target}, device_id_type=pl.DeviceIdType.MESH,
        )

    barrier = pltpu.get_barrier_semaphore()

    def greet(d, _):
        pl.semaphore_signal(
            barrier, inc=1, device_id={"inner": (inner + d) % N}, device_id_type=pl.DeviceIdType.MESH
        )
        pl.semaphore_signal(
            barrier, inc=1, device_id={"outer": (outer + d) % N}, device_id_type=pl.DeviceIdType.MESH
        )
        return 0

    lax.fori_loop(1, N, greet, 0)

    left = iota((1, 128), 1) < 64
    half_k = jnp.where(left, SCALE, 0.0).astype(BF)
    half_v = jnp.where(left, 0.0, 1.0).astype(BF)

    def order(step):
        return (step + inner) % (HEADS // 2)

    def pack(step, _):
        p = order(step)
        cols = pl.ds(pl.multiple_of(p * 128, 128), 128)
        qp, kp, vp, gp = q_ref[:, cols], k_ref[:, cols], v_ref[:, cols], g_ref[:, cols]
        for a in range(2):
            h = 2 * p + a
            lo, hi = 64 * a, 64 * a + 64
            x = jnp.concatenate([qp[:, lo:hi], gp[:, lo:hi]], axis=1)
            y = jnp.concatenate([kp[:, lo:hi], vp[:, lo:hi]], axis=1)
            xl[h] = x
            yl[h] = y
            om, ow = om_ref[h], ow_ref[h]
            row = iota((96, 1), 0)
            r = row - 64
            w = r & 15
            wide = jnp.where((r < 16) & (w < 4), 64 * w + ow, -1)
            wide = jnp.where((r >= 16) & (w >= 4) & (w < 8), 64 * (w - 4) + ow, wide)
            want = jnp.where(row < 64, 4 * row + om, wide)
            pick = onehot(iota((96, T), 1) == want)
            got = nn(pick, jnp.concatenate([x, y], axis=1))
            msg[h, 0:64, :] = got[0:64, 0:128].astype(BF)
            msg[h, 64:128, :] = got[0:64, 128:256].astype(BF)
            msg[h, 128:144, :] = (got[64:80, 0:128] + got[80:96, 128:256]).astype(BF)
        return 0

    lax.fori_loop(0, HEADS // 2, pack, 0)
    pl.semaphore_wait(barrier, 2 * (N - 1))

    def send_msg(step, _):
        h = (step + 2 * inner) % HEADS
        target = device_of(h)

        @pl.when(target != inner)
        def _():
            to_inner(msg.at[h], rx.at[inner], msg_s.at[h], msg_r.at[inner], target).start()

        @pl.when(target == inner)
        def _():
            rx[inner] = msg[h]

        return 0

    lax.fori_loop(0, HEADS, send_msg, 0)

    t_row = iota((T, 128), 0)
    t_lane = iota((T, 128), 1)
    place_m = onehot(t_lane == (t_row >> 2) + 64 * (inner % 2))
    place_w = onehot(t_lane == (t_row >> 6) + 4 * inner)
    tok = iota((1, T), 1)

    def local_a(p, _):
        cols = pl.ds(pl.multiple_of(p * 128, 128), 128)
        prod = g_ref[:, cols].astype(F32) * o_ref[:, cols].astype(F32)
        hi = prod.astype(BF)
        lo = (prod - hi.astype(F32)).astype(BF)
        halves = onehot(iota((16, 128), 0) == (iota((16, 128), 1) >> 6))
        delta = nt(halves, hi) + nt(halves, lo)
        tops, lses = [], []
        for a in range(2):
            h = 2 * p + a
            x, y = xl[h], yl[h]
            s = nt(y * half_k, x)
            top = jnp.max(s, axis=0, keepdims=True)
            e = jnp.exp(s - top)
            tops.append(top)
            lses.append(top + jnp.log(jnp.sum(e, axis=0, keepdims=True)))
            d = nt(y * half_v, x)
            el[h] = e.astype(BF)
            gl[h] = (e * (d - delta[a : a + 1])).astype(BF)
        row = iota((8, 1), 0)
        mst[p] = jnp.where(
            row < 2, jnp.where(row == 0, tops[0], tops[1]), jnp.where(row == 2, lses[0], lses[1])
        )
        first, wide = row < 4, (row & 2) != 0
        is_delta = (row & 1) == 0
        base = jnp.where(
            first,
            jnp.where(is_delta, delta[0:1], lses[0]),
            jnp.where(is_delta, delta[1:2], lses[1]),
        )
        off = jnp.where(
            first,
            jnp.where(wide, ow_ref[2 * p], om_ref[2 * p]),
            jnp.where(wide, ow_ref[2 * p + 1], om_ref[2 * p + 1]),
        )
        kept = (tok & jnp.where(wide, 63, 3)) == off
        parts = split3(jnp.where(kept, base, 0.0))
        st_tx[p] = jnp.where(wide, sum3(nn(parts, place_w)), sum3(nn(parts, place_m)))
        return 0

    lax.fori_loop(0, HEADS // 2, local_a, 0)

    def send_st(step, _):
        h = (step + 2 * inner) % HEADS
        target = device_of(h)

        @pl.when(target != inner)
        def _():
            to_inner(st_tx.at[h // 2], st_rx.at[inner], st_s.at[h], st_r.at[inner], target).start()

        @pl.when(target == inner)
        def _():
            st_rx[inner] = st_tx[h // 2]

        return 0

    lax.fori_loop(0, HEADS, send_st, 0)

    @pl.when(active)
    def _():
        def get_msg(i, _):
            @pl.when(i != inner)
            def _():
                to_inner(msg.at[0], rx.at[i], msg_s.at[0], msg_r.at[i], i).wait_recv()

            return 0

        lax.fori_loop(0, N, get_msg, 0)

        om, ow = om_ref[head], ow_ref[head]
        row64, col256 = iota((64, T), 0), iota((64, T), 1)
        at = 16 * (row64 >> 2) + (row64 & 3)
        wide_rows = rx[:, 128:144, :].reshape(T, 128)
        xw_w[...] = nn(onehot(col256 == at), wide_rows).astype(BF)
        yw[...] = nn(onehot(col256 == at + 4), wide_rows).astype(BF)
        rxo[outer] = yw[...]

        def send_yw(d, _):
            t = (outer + d) % N
            to_outer(yw, rxo.at[outer], yw_s.at[t], yw_r.at[outer], t).start()
            return 0

        lax.fori_loop(1, N, send_yw, 0)

        def get_st(i, _):
            @pl.when(i != inner)
            def _():
                to_inner(st_tx.at[0], st_rx.at[i], st_s.at[0], st_r.at[i], i).wait_recv()

            return 0

        lax.fori_loop(0, N, get_st, 0)

        even = head % 2 == 0

        def stat(index):
            return jnp.where(even, st_rx[:, index, :], st_rx[:, index + 4, :])

        def chunks(rows):
            pair = iota((8, N), 0) == (iota((8, N), 1) >> 1)
            return sum3_cols(pair, rows)

        def sum3_cols(pair, rows):
            a = rows.astype(BF).astype(F32)
            r = rows - a
            b = r.astype(BF).astype(F32)
            c = (r - b).astype(BF)
            ones = onehot(pair)
            return nn(ones, a.astype(BF)) + nn(ones, b.astype(BF)) + nn(ones, c)

        dm[...] = chunks(stat(0))
        lse_local_m = chunks(stat(1))
        delta_w = jnp.sum(stat(2), axis=0, keepdims=True)
        lse_local_w = jnp.sum(stat(3), axis=0, keepdims=True)

        def halves(i, _):
            y = rx[i, 64:128, :]
            yk[i] = y * half_k
            yv[i] = y * half_v
            return 0

        lax.fori_loop(0, N, halves, 0)

        def mid_a(b, _):
            x = rx[pl.ds(4 * b, 4), 0:64, :].reshape(T, 128)
            delta = jnp.concatenate([dm[pl.ds(2 * b, 1), :], dm[pl.ds(2 * b + 1, 1), :]], axis=1)
            top = jnp.full((1, T), NEG, F32)
            for kb in range(4):
                s = nt(yk[4 * kb : 4 * kb + 4].reshape(T, 128), x)
                s_scr[kb] = s
                top = jnp.maximum(top, jnp.max(s, axis=0, keepdims=True))
            total = jnp.zeros((1, T), F32)
            for kb in range(4):
                e = jnp.exp(s_scr[kb] - top)
                total = total + jnp.sum(e, axis=0, keepdims=True)
                d = nt(yv[4 * kb : 4 * kb + 4].reshape(T, 128), x)
                em[b, kb] = e.astype(BF)
                gm[b, kb] = (e * (d - delta)).astype(BF)
            lse = top + jnp.log(total)
            mm[pl.ds(2 * b, 1), :] = top[:, :128]
            mm[pl.ds(2 * b + 1, 1), :] = top[:, 128:]
            ml[pl.ds(2 * b, 1), :] = lse[:, :128]
            ml[pl.ds(2 * b + 1, 1), :] = lse[:, 128:]
            return 0

        lax.fori_loop(0, 4, mid_a, 0)

        def get_yw(i, _):
            @pl.when(i != outer)
            def _():
                to_outer(yw, rxo.at[i], yw_s.at[i], yw_r.at[i], i).wait_recv()

            return 0

        lax.fori_loop(0, N, get_yw, 0)

        all_y = rxo[...].reshape(N * 64, 128)
        x_w = xw_w[...]
        s = nt(all_y * half_k, x_w)
        top_w = jnp.max(s, axis=0, keepdims=True)
        e = jnp.exp(s - top_w)
        lse_w = top_w + jnp.log(jnp.sum(e, axis=0, keepdims=True))
        d = nt(all_y * half_v, x_w)
        ew = e.astype(BF)
        gw = (e * (d - delta_w[:, :64])).astype(BF)
        zeros64 = jnp.zeros((1, 64), F32)
        top_w = jnp.concatenate([top_w, zeros64], axis=1)
        lse_w = jnp.concatenate([lse_w, zeros64], axis=1)

        lse_m = ml[...]
        shared = (ow & 3) == om
        spot = jnp.where(shared, ow >> 2, -1)
        lane8, chunk8 = iota((8, 128), 1), iota((8, 128), 0)
        here = (lane8 & 15) == spot
        n128 = iota((128, 128), 1)
        spread = onehot(((n128 & 7) == (iota((128, 128), 0) >> 4)) & (n128 < 64))
        own = (lane8 >> 3) == chunk8
        m_at_w = sum3(nn(split3(jnp.where(here, lse_m, 0.0)), spread))
        m_at_w = jnp.sum(jnp.where(own, m_at_w, 0.0), axis=0, keepdims=True)
        w_at_m = sum3(nt(split3(jnp.where(own, lse_w, 0.0)), spread))
        total_m = lse3(lse_m, lse_local_m, jnp.where(here, w_at_m, NEG))
        spot_row = jnp.full((1, 128), spot, I32)
        total_w = lse3(lse_w, lse_local_w, jnp.where(spot_row >= 0, m_at_w, NEG))
        for j in range(8):
            ls_tx[j] = jnp.where(chunk8 == 0, lse_m[j : j + 1], lse_w)

        def send_ls(d, _):
            t = (inner + d) % N
            to_inner(ls_tx.at[t // 2], ls_rx.at[head], ls_s.at[t], ls_r.at[head], t).start()
            return 0

        lax.fori_loop(1, N, send_ls, 0)
        ls_rx[head] = ls_tx[inner // 2]

        weight_m = jnp.exp(mm[...] - total_m)
        weight_w = jnp.exp(top_w - total_w)
        stacked = jnp.concatenate(
            [weight_m, jnp.broadcast_to(weight_w, (8, 128)), jnp.zeros((112, 128), F32)], axis=0
        )
        columns = stacked.T

        col_w = columns[0:64, 8:9]
        scaled = (x_w.astype(F32) * col_w).astype(BF)
        wp[...] = jnp.where(left, nn(gw, scaled), nn(ew, scaled)).astype(BF).reshape(N, 64, 128)
        rxp[outer] = wp[outer]

        def send_wp(d, _):
            t = (outer + d) % N
            to_outer(wp.at[t], rxp.at[outer], wp_s.at[t], wp_r.at[outer], t).start()
            return 0

        lax.fori_loop(1, N, send_wp, 0)
        dq_w = (tn(gw, all_y) * col_w).astype(BF)

        for j in range(8):
            x = rx[2 * j : 2 * j + 2, 0:64, :].reshape(128, 128).astype(F32)
            col = columns[:, j : j + 1]
            xw_all[128 * j : 128 * j + 128, :] = (x * col).astype(BF)
            acc_q[0, 128 * j % 256 : 128 * j % 256 + 128, :] = jnp.broadcast_to(col, (128, 128))
            if j % 2 == 1:
                b = j // 2
                g_k = jnp.zeros((T, 128), F32)
                for kb in range(4):
                    g_k = g_k + tn(gm[b, kb], rx[4 * kb : 4 * kb + 4, 64:128, :].reshape(T, 128))
                g_k = g_k * acc_q[0]
                for i in range(4):
                    mine = g_k[64 * i : 64 * i + 64]
                    ret[4 * b + i, 64:96, :] = jnp.where(left, mine[:32], swap(mine[32:])).astype(BF)

        def mid_b(kb, _):
            from_g = jnp.zeros((T, 128), F32)
            from_e = jnp.zeros((T, 128), F32)
            for b in range(4):
                x = xw_all[256 * b : 256 * b + 256, :]
                from_g = from_g + nn(gm[b, kb], x)
                from_e = from_e + nn(em[b, kb], x)
            both = jnp.where(left, from_g, from_e).astype(BF)
            ret[pl.ds(4 * kb, 4), 0:64, :] = both.reshape(4, 64, 128)
            for i in range(4):
                t = 4 * kb + i

                @pl.when(t != inner)
                def _():
                    to_inner(ret.at[t], ret_rx.at[head], ret_s.at[t], ret_r.at[head], t).start()

            return 0

        lax.fori_loop(0, 4, mid_b, 0)
        ret_rx[head] = ret[inner]

        def get_wp(i, total):
            @pl.when(i != outer)
            def _():
                to_outer(wp.at[0], rxp.at[i], wp_s.at[0], wp_r.at[i], i).wait_recv()

            return total + rxp[i].astype(F32)

        kv_w = lax.fori_loop(0, N, get_wp, jnp.zeros((64, 128), F32)).astype(BF)
        r256, n64 = iota((T, 64), 0), iota((T, 64), 1)
        slot = r256 & 15
        at = 4 * (r256 >> 4) + (slot & 3)
        back = nn(onehot((n64 == at) & (slot < 4)), kv_w)
        back = back + nn(onehot((n64 == at) & (slot >= 4) & (slot < 8)), dq_w)
        retw[...] = back.astype(BF).reshape(N, 16, 128)

        def send_retw(d, _):
            t = (inner + d) % N
            to_inner(retw.at[t], retw_rx.at[head], retw_s.at[t], retw_r.at[head], t).start()
            return 0

        lax.fori_loop(1, N, send_retw, 0)
        retw_rx[head] = retw[inner]

    def get_ls(h, _):
        t = device_of(h)

        @pl.when(t != inner)
        def _():
            to_inner(ls_tx.at[0], ls_rx.at[h], ls_s.at[0], ls_r.at[h], t).wait_recv()

        return 0

    lax.fori_loop(0, HEADS, get_ls, 0)

    def local_b(p, _):
        row = iota((8, 1), 0)
        first, second = ls_rx[2 * p], ls_rx[2 * p + 1]
        rows = jnp.where(
            row < 2,
            jnp.where(row == 0, first[0:1], second[0:1]),
            jnp.where(row == 2, first[1:2], second[1:2]),
        )
        parts = split3(rows)
        lse_m = sum3(nt(parts, place_m))[0:2]
        lse_w = sum3(nt(parts, place_w))[2:4]
        top, lse = mst[p][0:2], mst[p][2:4]
        row2 = iota((2, 1), 0)
        om = jnp.where(row2 == 0, om_ref[2 * p], om_ref[2 * p + 1])
        ow = jnp.where(row2 == 0, ow_ref[2 * p], ow_ref[2 * p + 1])
        total = lse3(
            lse, jnp.where((tok & 3) == om, lse_m, NEG), jnp.where((tok & 63) == ow, lse_w, NEG)
        )
        weight = jnp.exp(top - total)
        r128 = iota((128, 1), 0)
        columns = jnp.where(r128 == 0, weight[0:1], weight[1:2]).T
        for a in range(2):
            h = 2 * p + a
            col = columns[:, a : a + 1]
            x = (xl[h].astype(F32) * col).astype(BF)
            acc_kv[h] = jnp.where(left, nn(gl[h], x), nn(el[h], x))
            acc_q[h] = tn(gl[h], yl[h]) * col
        return 0

    lax.fori_loop(0, HEADS // 2, local_b, 0)

    def get_ret(h, _):
        t = device_of(h)

        @pl.when(t != inner)
        def _():
            to_inner(ret.at[0], ret_rx.at[h], ret_s.at[0], ret_r.at[h], t).wait_recv()
            to_inner(retw.at[0], retw_rx.at[h], retw_s.at[0], retw_r.at[h], t).wait_recv()

        return 0

    lax.fori_loop(0, HEADS, get_ret, 0)

    def finish(p, _):
        cols = pl.ds(pl.multiple_of(p * 128, 128), 128)
        kvs, qs, rest = [], [], []
        for a in range(2):
            h = 2 * p + a
            om, ow = om_ref[h], ow_ref[h]
            r = iota((1, 112), 1)
            t = iota((T, 112), 0)
            back = jnp.concatenate([ret_rx[h], retw_rx[h]], axis=0)
            want_kv = jnp.where(r < 64, 4 * r + om, jnp.where((r >= 96) & (r < 100), 64 * (r - 96) + ow, -1))
            in_q = (r >= 64) & (r < 96)
            want_q = jnp.where(
                in_q, 4 * (r - 64) + om, jnp.where((r >= 100) & (r < 104), 64 * (r - 100) + ow, -1)
            )
            want_r = jnp.where(in_q, 4 * (r - 32) + om, -1)
            kvs.append(acc_kv[h] + nn(onehot(t == want_kv), back))
            qs.append(acc_q[h] + nn(onehot(t == want_q), back))
            rest.append(nn(onehot(t == want_r), back))
        dq = jnp.where(left, qs[0] + swap(rest[0]), swap(qs[1]) + rest[1])
        dq_ref[:, cols] = (SCALE * dq).astype(BF)
        dk_ref[:, cols] = (SCALE * jnp.where(left, kvs[0], swap(kvs[1]))).astype(BF)
        dv_ref[:, cols] = jnp.where(left, swap(kvs[0]), kvs[1]).astype(BF)
        return 0

    lax.fori_loop(0, HEADS // 2, finish, 0)

    def sent_heads(h, _):
        t = device_of(h)

        @pl.when(t != inner)
        def _():
            to_inner(msg.at[h], rx.at[inner], msg_s.at[h], msg_r.at[inner], t).wait_send()
            to_inner(st_tx.at[h // 2], st_rx.at[inner], st_s.at[h], st_r.at[inner], t).wait_send()

        return 0

    lax.fori_loop(0, HEADS, sent_heads, 0)

    @pl.when(active)
    def _():
        def sent(d, _):
            t = (inner + d) % N
            to_inner(ls_tx.at[t // 2], ls_rx.at[head], ls_s.at[t], ls_r.at[head], t).wait_send()
            to_inner(ret.at[t], ret_rx.at[head], ret_s.at[t], ret_r.at[head], t).wait_send()
            to_inner(retw.at[t], retw_rx.at[head], retw_s.at[t], retw_r.at[head], t).wait_send()
            t = (outer + d) % N
            to_outer(yw, rxo.at[outer], yw_s.at[t], yw_r.at[outer], t).wait_send()
            to_outer(wp.at[t], rxp.at[outer], wp_s.at[t], wp_r.at[outer], t).wait_send()
            return 0

        lax.fori_loop(1, N, sent, 0)


def per_device(queries, keys, values, saved_out, out_grad, offset_mid, offset_wide):
    out = jax.ShapeDtypeStruct((T, HEADS * 64), BF)
    vmem = pl.BlockSpec(memory_space=pltpu.VMEM)
    smem = pl.BlockSpec(memory_space=pltpu.SMEM)
    v = pltpu.VMEM
    dma = pltpu.SemaphoreType.DMA
    return pl.pallas_call(
        kernel,
        out_shape=(out, out, out),
        in_specs=[smem, smem] + [vmem] * 5,
        out_specs=(vmem, vmem, vmem),
        scratch_shapes=[
            v((HEADS, T, 128), BF),
            v((HEADS, T, 128), BF),
            v((HEADS, MSG, 128), BF),
            v((N, MSG, 128), BF),
            v((HEADS, T, T), BF),
            v((HEADS, T, T), BF),
            v((HEADS // 2, 8, T), F32),
            v((HEADS // 2, 8, 128), F32),
            v((N, 8, 128), F32),
            v((8, 8, 128), F32),
            v((HEADS, 8, 128), F32),
            v((N, 64, 128), BF),
            v((N, 64, 128), BF),
            v((4, T, T), F32),
            v((4, 4, T, T), BF),
            v((4, 4, T, T), BF),
            v((8, 128), F32),
            v((8, 128), F32),
            v((8, 128), F32),
            v((N * 64, 128), BF),
            v((64, 128), BF),
            v((64, 128), BF),
            v((N, 64, 128), BF),
            v((N, 64, 128), BF),
            v((N, 64, 128), BF),
            v((N, RET, 128), BF),
            v((N, 16, 128), BF),
            v((HEADS, RET, 128), BF),
            v((HEADS, 16, 128), BF),
            v((HEADS, T, 128), F32),
            v((HEADS, T, 128), F32),
            dma((HEADS,)), dma((N,)),
            dma((HEADS,)), dma((N,)),
            dma((N,)), dma((HEADS,)),
            dma((N,)), dma((N,)),
            dma((N,)), dma((N,)),
            dma((N,)), dma((HEADS,)),
            dma((N,)), dma((HEADS,)),
        ],
        compiler_params=pltpu.CompilerParams(
            collective_id=0, has_side_effects=True, vmem_limit_bytes=48 * 1024 * 1024
        ),
    )(offset_mid, offset_wide, queries, keys, values, saved_out, out_grad)


def solution(mesh):
    rows = P(("outer", "inner"), None)
    return jax.shard_map(
        per_device,
        mesh=mesh,
        in_specs=(rows, rows, rows, rows, rows, P(), P()),
        out_specs=(rows, rows, rows),
        check_vma=False,
    )
```

time: 2290 us -> 63.5 us (0.03)
  waiting for transfers between devices: 2100 us -> 0 us
  local copies, waits for them, and re-layouts: 122 us -> 8.52 us
  Pallas kernels: 0 us -> 54 us
  matrix products: 32.6 us -> 0 us
    all_gather x4 -> x0, waiting for transfers between devices: 1460 us -> none  [the longest x1 681 us: per_device(): lax.all_gather(flatten(key_wide), ('outer', 'inner'), axis=0, tiled=True)]
    unnamed x10 -> x0, waiting for transfers between devices: 645 us -> none
    pallas_call x0 -> x1, Pallas kernels: none -> 54 us  [per_device(): pl.pallas_call(kernel, out_shape=(out, out, out), in_specs=[smem, smem] +...]
    broadcast_in_dim x22 -> x0, local copies, waits for them, and re-layouts: 40.7 us -> none  [spread_rows(): jnp.where(chosen[:, :, None], jnp.expand_dims(picked, -3), jnp.zeros((),...]
    dot_general x15 -> x0, matrix products: 32.6 us -> none  [the longest x3 8.63 us: branch_grads(): jnp.einsum('rpj,xpj->prx', output_gradient, values, preferred_element_typ...]
    unnamed x73 -> x17, local copies, waits for them, and re-layouts: 32.4 us -> 8.52 us
  transfers between devices with their start and end apart: 7 -> 0, of which waited for: 7 -> 0; matrix products, arithmetic and copies ran while one was open for 6% -> 0% of each run, Pallas kernels for 0% -> 0%
where the time goes in v1:
time: 63.5 us; the launch traced here: 63.2 us
  Pallas kernels  54 us (85%)
  local copies, waits for them, and re-layouts  8.52 us (13%)
  between operations  0.66 us (1%)
    pallas_call x1, Pallas kernels, per_device(): pl.pallas_call(kernel, out_shape=(out, out, out), in_specs=[smem, smem] +...  54 us
    unnamed x17, local copies, waits for them, and re-layouts  8.52 us

profile of v1, /device:TPU:1, one launch (start us, length us, event | category | flops | bytes accessed | tf_op | source)
XLA Modules:
  0.0 63.2 jit_solution(8139219838211999756)
XLA Ops:
  0.6 0.0 copy-start
  0.6 1.0 %copy-done = bf16[256,768]{1,0:T(8,128)(2,1)S(1)} copy-done((bf16[256,768]{1,0:T(8,128)(2,1)S(1)}, bf16[256,768]{1,0:T(8,128)(2,1)}, u32[]{:S(2)}) %copy-start) | copy-done | bytes 393240
  1.6 0.0 copy-start.1
  1.6 1.0 %copy-done.1 = bf16[256,768]{1,0:T(8,128)(2,1)S(1)} copy-done((bf16[256,768]{1,0:T(8,128)(2,1)S(1)}, bf16[256,768]{1,0:T(8,128)(2,1)}, u32[]{:S(2)}) %copy-start.1) | copy-done | bytes 393240
  2.6 0.0 copy-start.2
  2.6 1.0 %copy-done.2 = bf16[256,768]{1,0:T(8,128)(2,1)S(1)} copy-done((bf16[256,768]{1,0:T(8,128)(2,1)S(1)}, bf16[256,768]{1,0:T(8,128)(2,1)}, u32[]{:S(2)}) %copy-start.2) | copy-done | bytes 393240
  3.6 0.0 copy-start.3
  3.6 1.0 %copy-done.3 = bf16[256,768]{1,0:T(8,128)(2,1)S(1)} copy-done((bf16[256,768]{1,0:T(8,128)(2,1)S(1)}, bf16[256,768]{1,0:T(8,128)(2,1)}, u32[]{:S(2)}) %copy-start.3) | copy-done | bytes 393240
  4.6 0.0 copy-start.4
  4.6 1.0 %copy-done.4 = bf16[256,768]{1,0:T(8,128)(2,1)S(1)} copy-done((bf16[256,768]{1,0:T(8,128)(2,1)S(1)}, bf16[256,768]{1,0:T(8,128)(2,1)}, u32[]{:S(2)}) %copy-start.4) | copy-done | bytes 393240
  5.6 0.0 copy-start.5
  5.6 0.7 %copy-done.5 = s32[12]{0:T(128)S(1)} copy-done((s32[12]{0:T(128)S(1)}, s32[12]{0:T(128)}, u32[]{:S(2)}) %copy-start.5) | copy-done | bytes 72
  6.3 0.0 copy-start.6
  6.3 0.7 %copy-done.6 = s32[12]{0:T(128)S(1)} copy-done((s32[12]{0:T(128)S(1)}, s32[12]{0:T(128)}, u32[]{:S(2)}) %copy-start.6) | copy-done | bytes 72
  6.9 54.0 %shard_map.94 = (bf16[256,768]{1,0:T(8,128)(2,1)S(1)}, bf16[256,768]{1,0:T(8,128)(2,1)S(1)}, bf16[256,768]{1,0:T(8,128)(2,1)S(1)}) custom-call(s32[12]{0:T(128)S(1)} %copy-done.5, s32[12]{0:T(128)S(1)} %copy-done.6, bf16[256,768]{1,0:T(8,128)(2,1)S(1)} %copy-done, bf16[256,768]{1,0:T(8,128)(2,1)S(1)} %copy-done.1, bf16[256,768]{1,0:T(8,128)(2,1)S(1)} %copy-done.2, ...), custom_call_target="tpu_custom_call" | custom-call | tf_op jit(solution)/shard_map/pallas_call | solution.py:548
  60.9 0.7 %copy.13 = bf16[256,768]{1,0:T(8,128)(2,1)} copy(bf16[256,768]{1,0:T(8,128)(2,1)S(1)} %get-tuple-element.6) | data formatting | bytes 786432
  61.7 0.7 %copy.14 = bf16[256,768]{1,0:T(8,128)(2,1)} copy(bf16[256,768]{1,0:T(8,128)(2,1)S(1)} %get-tuple-element.7) | data formatting | bytes 786432
  62.4 0.7 %copy.15 = bf16[256,768]{1,0:T(8,128)(2,1)} copy(bf16[256,768]{1,0:T(8,128)(2,1)S(1)} %get-tuple-element.8) | data formatting | bytes 786432
Async XLA Ops:
  0.6 1.0 %copy-start = (bf16[256,768]{1,0:T(8,128)(2,1)S(1)}, bf16[256,768]{1,0:T(8,128)(2,1)}, u32[]{:S(2)}) copy-start(bf16[256,768]{1,0:T(8,128)(2,1)} %q_ref.1) | copy-start | bytes 1179652
  1.6 1.0 %copy-start.1 = (bf16[256,768]{1,0:T(8,128)(2,1)S(1)}, bf16[256,768]{1,0:T(8,128)(2,1)}, u32[]{:S(2)}) copy-start(bf16[256,768]{1,0:T(8,128)(2,1)} %k_ref.1) | copy-start | bytes 1179652
  2.6 1.0 %copy-start.2 = (bf16[256,768]{1,0:T(8,128)(2,1)S(1)}, bf16[256,768]{1,0:T(8,128)(2,1)}, u32[]{:S(2)}) copy-start(bf16[256,768]{1,0:T(8,128)(2,1)} %v_ref.1) | copy-start | bytes 1179652
  3.6 1.0 %copy-start.3 = (bf16[256,768]{1,0:T(8,128)(2,1)S(1)}, bf16[256,768]{1,0:T(8,128)(2,1)}, u32[]{:S(2)}) copy-start(bf16[256,768]{1,0:T(8,128)(2,1)} %o_ref.1) | copy-start | bytes 1179652
  4.6 1.0 %copy-start.4 = (bf16[256,768]{1,0:T(8,128)(2,1)S(1)}, bf16[256,768]{1,0:T(8,128)(2,1)}, u32[]{:S(2)}) copy-start(bf16[256,768]{1,0:T(8,128)(2,1)} %g_ref.1) | copy-start | bytes 1179652
  5.6 0.7 %copy-start.5 = (s32[12]{0:T(128)S(1)}, s32[12]{0:T(128)}, u32[]{:S(2)}) copy-start(s32[12]{0:T(128)} %om_ref.1) | copy-start | bytes 148
  6.3 0.7 %copy-start.6 = (s32[12]{0:T(128)S(1)}, s32[12]{0:T(128)}, u32[]{:S(2)}) copy-start(s32[12]{0:T(128)} %ow_ref.1) | copy-start | bytes 148

commit v2 on v1

--- a/solution.py
+++ b/solution.py
@@ -15,8 +15,7 @@
 MID = 64
 SCALE = 0.125
 NEG = -1e30
-MSG = 144
-RET = 96
+BACK = 112
 
 
 def iota(shape, dim):
@@ -65,17 +64,19 @@
 
 
 def kernel(
+    om_hbm, ow_hbm, q_hbm, k_hbm, v_hbm, o_hbm, g_hbm,
+    acc_kv, acc_q, back, where_back,
     om_ref, ow_ref, q_ref, k_ref, v_ref, o_ref, g_ref,
-    dq_ref, dk_ref, dv_ref,
-    xl, yl, msg, rx, el, gl, mst, st_tx, st_rx, ls_tx, ls_rx,
-    yk, yv, s_scr, em, gm, mm, ml, dm, xw_all, xw_w, yw, rxo, wp, rxp,
-    ret, retw, ret_rx, retw_rx, acc_kv, acc_q,
-    msg_s, msg_r, st_s, st_r, ls_s, ls_r, yw_s, yw_r, wp_s, wp_r, ret_s, ret_r, retw_s, retw_r,
+    xl, yl, msg_w, msg_k, msg_q, rx_w, rx_k, rx_q, el, gl, mst, st_tx, st_rx, ls_tx, ls_rx,
+    yk, yv, s_scr, em, gm, mm, ml, dm, dq_m, xw_all, xw_w, yw, rxo, wp, rxp, ret, retw,
+    in_s, mw_s, mw_r, mk_s, mk_r, mq_s, mq_r, st_s, st_r, ls_s, ls_r, yw_s, yw_r, wp_s, wp_r,
+    rk_s, rk_r, rq_s, rq_r, rw_s, rw_r,
 ):
     inner = lax.axis_index("inner")
     outer = lax.axis_index("outer")
+    quad = inner // 4
     active = inner % 4 < 3
-    head = jnp.minimum((inner // 4) * 3 + inner % 4, HEADS - 1)
+    head = jnp.minimum(quad * 3 + inner % 4, HEADS - 1)
 
     def to_inner(src, dst, send, recv, target):
         return pltpu.make_async_remote_copy(
@@ -89,6 +90,18 @@
             device_id={"outer": target}, device_id_type=pl.DeviceIdType.MESH,
         )
 
+    loads = [
+        pltpu.make_async_copy(src, dst, in_s.at[i])
+        for i, (src, dst) in enumerate(
+            [
+                (om_hbm, om_ref), (ow_hbm, ow_ref), (q_hbm, q_ref), (g_hbm, g_ref),
+                (k_hbm, k_ref), (v_hbm, v_ref), (o_hbm, o_ref),
+            ]
+        )
+    ]
+    for load in loads:
+        load.start()
+
     barrier = pltpu.get_barrier_semaphore()
 
     def greet(d, _):
@@ -101,16 +114,14 @@
         return 0
 
     lax.fori_loop(1, N, greet, 0)
+    for load in loads[:6]:
+        load.wait()
 
     left = iota((1, 128), 1) < 64
     half_k = jnp.where(left, SCALE, 0.0).astype(BF)
     half_v = jnp.where(left, 0.0, 1.0).astype(BF)
 
-    def order(step):
-        return (step + inner) % (HEADS // 2)
-
-    def pack(step, _):
-        p = order(step)
+    def pack(p, _):
         cols = pl.ds(pl.multiple_of(p * 128, 128), 128)
         qp, kp, vp, gp = q_ref[:, cols], k_ref[:, cols], v_ref[:, cols], g_ref[:, cols]
         for a in range(2):
@@ -129,35 +140,44 @@
             want = jnp.where(row < 64, 4 * row + om, wide)
             pick = onehot(iota((96, T), 1) == want)
             got = nn(pick, jnp.concatenate([x, y], axis=1))
-            msg[h, 0:64, :] = got[0:64, 0:128].astype(BF)
-            msg[h, 64:128, :] = got[0:64, 128:256].astype(BF)
-            msg[h, 128:144, :] = (got[64:80, 0:128] + got[80:96, 128:256]).astype(BF)
+            msg_q[h] = got[0:64, 0:128].astype(BF)
+            msg_k[h] = got[0:64, 128:256].astype(BF)
+            msg_w[h] = (got[64:80, 0:128] + got[80:96, 128:256]).astype(BF)
         return 0
 
     lax.fori_loop(0, HEADS // 2, pack, 0)
     pl.semaphore_wait(barrier, 2 * (N - 1))
 
-    def send_msg(step, _):
-        h = (step + 2 * inner) % HEADS
-        target = device_of(h)
-
-        @pl.when(target != inner)
-        def _():
-            to_inner(msg.at[h], rx.at[inner], msg_s.at[h], msg_r.at[inner], target).start()
-
-        @pl.when(target == inner)
-        def _():
-            rx[inner] = msg[h]
-
-        return 0
-
-    lax.fori_loop(0, HEADS, send_msg, 0)
+    def send_to_heads(src_of, dst, send, recv):
+        def step(i, _):
+            block = (quad + i // 3) % 4
+            j = (i + inner) % 3
+            h, target = 3 * block + j, 4 * block + j
+
+            @pl.when(target != inner)
+            def _():
+                to_inner(src_of(h), dst.at[inner], send.at[h], recv.at[inner], target).start()
+
+            return 0
+
+        lax.fori_loop(0, HEADS, step, 0)
+
+    send_to_heads(lambda h: msg_w.at[h], rx_w, mw_s, mw_r)
+    send_to_heads(lambda h: msg_k.at[h], rx_k, mk_s, mk_r)
+    send_to_heads(lambda h: msg_q.at[h], rx_q, mq_s, mq_r)
+
+    @pl.when(active)
+    def _():
+        rx_w[inner] = msg_w[head]
+        rx_k[inner] = msg_k[head]
+        rx_q[inner] = msg_q[head]
 
     t_row = iota((T, 128), 0)
     t_lane = iota((T, 128), 1)
     place_m = onehot(t_lane == (t_row >> 2) + 64 * (inner % 2))
     place_w = onehot(t_lane == (t_row >> 6) + 4 * inner)
     tok = iota((1, T), 1)
+    loads[6].wait()
 
     def local_a(p, _):
         cols = pl.ds(pl.multiple_of(p * 128, 128), 128)
@@ -200,38 +220,23 @@
         return 0
 
     lax.fori_loop(0, HEADS // 2, local_a, 0)
-
-    def send_st(step, _):
-        h = (step + 2 * inner) % HEADS
-        target = device_of(h)
-
-        @pl.when(target != inner)
-        def _():
-            to_inner(st_tx.at[h // 2], st_rx.at[inner], st_s.at[h], st_r.at[inner], target).start()
-
-        @pl.when(target == inner)
-        def _():
-            st_rx[inner] = st_tx[h // 2]
-
-        return 0
-
-    lax.fori_loop(0, HEADS, send_st, 0)
+    send_to_heads(lambda h: st_tx.at[h // 2], st_rx, st_s, st_r)
 
     @pl.when(active)
     def _():
-        def get_msg(i, _):
+        st_rx[inner] = st_tx[head // 2]
+
+        def get_wide(i, _):
             @pl.when(i != inner)
             def _():
-                to_inner(msg.at[0], rx.at[i], msg_s.at[0], msg_r.at[i], i).wait_recv()
-
-            return 0
-
-        lax.fori_loop(0, N, get_msg, 0)
-
-        om, ow = om_ref[head], ow_ref[head]
+                to_inner(msg_w.at[0], rx_w.at[i], mw_s.at[0], mw_r.at[i], i).wait_recv()
+
+            return 0
+
+        lax.fori_loop(0, N, get_wide, 0)
         row64, col256 = iota((64, T), 0), iota((64, T), 1)
         at = 16 * (row64 >> 2) + (row64 & 3)
-        wide_rows = rx[:, 128:144, :].reshape(T, 128)
+        wide_rows = rx_w[...].reshape(T, 128)
         xw_w[...] = nn(onehot(col256 == at), wide_rows).astype(BF)
         yw[...] = nn(onehot(col256 == at + 4), wide_rows).astype(BF)
         rxo[outer] = yw[...]
@@ -242,6 +247,38 @@
             return 0
 
         lax.fori_loop(1, N, send_yw, 0)
+
+    def local_q(h, _):
+        acc_q[h] = tn(gl[h], yl[h])
+        om, ow = om_ref[h], ow_ref[h]
+        r = iota((1, BACK), 1)
+        t = iota((T, BACK), 0)
+        in_q = (r >= 64) & (r < 96)
+        want_kv = jnp.where(r < 64, 4 * r + om, jnp.where((r >= 96) & (r < 100), 64 * (r - 96) + ow, -1))
+        want_q = jnp.where(
+            in_q, 4 * (r - 64) + om, jnp.where((r >= 100) & (r < 104), 64 * (r - 100) + ow, -1)
+        )
+        want_r = jnp.where(in_q, 4 * (r - 32) + om, -1)
+        where_back[h, 0] = onehot(t == want_kv)
+        where_back[h, 1] = onehot(t == want_q)
+        where_back[h, 2] = onehot(t == want_r)
+        return 0
+
+    lax.fori_loop(0, HEADS, local_q, 0)
+
+    @pl.when(active)
+    def _():
+        def get_keys(i, _):
+            @pl.when(i != inner)
+            def _():
+                to_inner(msg_k.at[0], rx_k.at[i], mk_s.at[0], mk_r.at[i], i).wait_recv()
+
+            y = rx_k[i]
+            yk[i] = y * half_k
+            yv[i] = y * half_v
+            return 0
+
+        lax.fori_loop(0, N, get_keys, 0)
 
         def get_st(i, _):
             @pl.when(i != inner)
@@ -252,21 +289,18 @@
 
         lax.fori_loop(0, N, get_st, 0)
 
+        om, ow = om_ref[head], ow_ref[head]
         even = head % 2 == 0
 
         def stat(index):
             return jnp.where(even, st_rx[:, index, :], st_rx[:, index + 4, :])
 
         def chunks(rows):
-            pair = iota((8, N), 0) == (iota((8, N), 1) >> 1)
-            return sum3_cols(pair, rows)
-
-        def sum3_cols(pair, rows):
+            ones = onehot(iota((8, N), 0) == (iota((8, N), 1) >> 1))
             a = rows.astype(BF).astype(F32)
             r = rows - a
             b = r.astype(BF).astype(F32)
             c = (r - b).astype(BF)
-            ones = onehot(pair)
             return nn(ones, a.astype(BF)) + nn(ones, b.astype(BF)) + nn(ones, c)
 
         dm[...] = chunks(stat(0))
@@ -274,16 +308,20 @@
         delta_w = jnp.sum(stat(2), axis=0, keepdims=True)
         lse_local_w = jnp.sum(stat(3), axis=0, keepdims=True)
 
-        def halves(i, _):
-            y = rx[i, 64:128, :]
-            yk[i] = y * half_k
-            yv[i] = y * half_v
-            return 0
-
-        lax.fori_loop(0, N, halves, 0)
-
-        def mid_a(b, _):
-            x = rx[pl.ds(4 * b, 4), 0:64, :].reshape(T, 128)
+        def mid_a(u, _):
+            b = (quad + 4 - u) % 4
+
+            def get_queries(j, _):
+                i = 4 * b + j
+
+                @pl.when(i != inner)
+                def _():
+                    to_inner(msg_q.at[0], rx_q.at[i], mq_s.at[0], mq_r.at[i], i).wait_recv()
+
+                return 0
+
+            lax.fori_loop(0, 4, get_queries, 0)
+            x = rx_q[pl.ds(4 * b, 4)].reshape(T, 128)
             delta = jnp.concatenate([dm[pl.ds(2 * b, 1), :], dm[pl.ds(2 * b + 1, 1), :]], axis=1)
             top = jnp.full((1, T), NEG, F32)
             for kb in range(4):
@@ -291,12 +329,16 @@
                 s_scr[kb] = s
                 top = jnp.maximum(top, jnp.max(s, axis=0, keepdims=True))
             total = jnp.zeros((1, T), F32)
+            dq = jnp.zeros((T, 128), F32)
             for kb in range(4):
                 e = jnp.exp(s_scr[kb] - top)
                 total = total + jnp.sum(e, axis=0, keepdims=True)
                 d = nt(yv[4 * kb : 4 * kb + 4].reshape(T, 128), x)
                 em[b, kb] = e.astype(BF)
-                gm[b, kb] = (e * (d - delta)).astype(BF)
+                g = (e * (d - delta)).astype(BF)
+                gm[b, kb] = g
+                dq = dq + tn(g, rx_k[4 * kb : 4 * kb + 4].reshape(T, 128))
+            dq_m[b] = dq
             lse = top + jnp.log(total)
             mm[pl.ds(2 * b, 1), :] = top[:, :128]
             mm[pl.ds(2 * b + 1, 1), :] = top[:, 128:]
@@ -374,21 +416,25 @@
         dq_w = (tn(gw, all_y) * col_w).astype(BF)
 
         for j in range(8):
-            x = rx[2 * j : 2 * j + 2, 0:64, :].reshape(128, 128).astype(F32)
             col = columns[:, j : j + 1]
+            x = rx_q[2 * j : 2 * j + 2].reshape(128, 128).astype(F32)
             xw_all[128 * j : 128 * j + 128, :] = (x * col).astype(BF)
-            acc_q[0, 128 * j % 256 : 128 * j % 256 + 128, :] = jnp.broadcast_to(col, (128, 128))
-            if j % 2 == 1:
-                b = j // 2
-                g_k = jnp.zeros((T, 128), F32)
-                for kb in range(4):
-                    g_k = g_k + tn(gm[b, kb], rx[4 * kb : 4 * kb + 4, 64:128, :].reshape(T, 128))
-                g_k = g_k * acc_q[0]
-                for i in range(4):
-                    mine = g_k[64 * i : 64 * i + 64]
-                    ret[4 * b + i, 64:96, :] = jnp.where(left, mine[:32], swap(mine[32:])).astype(BF)
-
-        def mid_b(kb, _):
+            dq = dq_m[j // 2, 128 * (j % 2) : 128 * (j % 2) + 128, :] * col
+            for i in range(2):
+                mine = dq[64 * i : 64 * i + 64]
+                ret[2 * j + i, 64:96, :] = jnp.where(left, mine[:32], swap(mine[32:])).astype(BF)
+
+        def send_rq(d, _):
+            t = (inner + d) % N
+            to_inner(
+                ret.at[t, pl.ds(64, 32)], back.at[head, pl.ds(64, 32)], rq_s.at[t], rq_r.at[head], t
+            ).start()
+            return 0
+
+        lax.fori_loop(1, N, send_rq, 0)
+
+        def mid_b(u, _):
+            kb = (quad + u) % 4
             from_g = jnp.zeros((T, 128), F32)
             from_e = jnp.zeros((T, 128), F32)
             for b in range(4):
@@ -397,17 +443,23 @@
                 from_e = from_e + nn(em[b, kb], x)
             both = jnp.where(left, from_g, from_e).astype(BF)
             ret[pl.ds(4 * kb, 4), 0:64, :] = both.reshape(4, 64, 128)
-            for i in range(4):
-                t = 4 * kb + i
+
+            def send_rk(j, _):
+                t = 4 * kb + (inner + j) % 4
 
                 @pl.when(t != inner)
                 def _():
-                    to_inner(ret.at[t], ret_rx.at[head], ret_s.at[t], ret_r.at[head], t).start()
-
+                    to_inner(
+                        ret.at[t, pl.ds(0, 64)], back.at[head, pl.ds(0, 64)], rk_s.at[t], rk_r.at[head], t
+                    ).start()
+
+                return 0
+
+            lax.fori_loop(0, 4, send_rk, 0)
             return 0
 
         lax.fori_loop(0, 4, mid_b, 0)
-        ret_rx[head] = ret[inner]
+        back[head, 0:96, :] = ret[inner]
 
         def get_wp(i, total):
             @pl.when(i != outer)
@@ -420,17 +472,17 @@
         r256, n64 = iota((T, 64), 0), iota((T, 64), 1)
         slot = r256 & 15
         at = 4 * (r256 >> 4) + (slot & 3)
-        back = nn(onehot((n64 == at) & (slot < 4)), kv_w)
-        back = back + nn(onehot((n64 == at) & (slot >= 4) & (slot < 8)), dq_w)
-        retw[...] = back.astype(BF).reshape(N, 16, 128)
-
-        def send_retw(d, _):
+        rows_w = nn(onehot((n64 == at) & (slot < 4)), kv_w)
+        rows_w = rows_w + nn(onehot((n64 == at) & (slot >= 4) & (slot < 8)), dq_w)
+        retw[...] = rows_w.astype(BF).reshape(N, 16, 128)
+
+        def send_rw(d, _):
             t = (inner + d) % N
-            to_inner(retw.at[t], retw_rx.at[head], retw_s.at[t], retw_r.at[head], t).start()
-            return 0
-
-        lax.fori_loop(1, N, send_retw, 0)
-        retw_rx[head] = retw[inner]
+            to_inner(retw.at[t], back.at[head, pl.ds(96, 16)], rw_s.at[t], rw_r.at[head], t).start()
+            return 0
+
+        lax.fori_loop(1, N, send_rw, 0)
+        back[head, 96:112, :] = retw[inner]
 
     def get_ls(h, _):
         t = device_of(h)
@@ -469,68 +521,44 @@
             col = columns[:, a : a + 1]
             x = (xl[h].astype(F32) * col).astype(BF)
             acc_kv[h] = jnp.where(left, nn(gl[h], x), nn(el[h], x))
-            acc_q[h] = tn(gl[h], yl[h]) * col
+            acc_q[h] = acc_q[h] * col
         return 0
 
     lax.fori_loop(0, HEADS // 2, local_b, 0)
 
-    def get_ret(h, _):
+    def get_back(h, _):
         t = device_of(h)
 
         @pl.when(t != inner)
         def _():
-            to_inner(ret.at[0], ret_rx.at[h], ret_s.at[0], ret_r.at[h], t).wait_recv()
-            to_inner(retw.at[0], retw_rx.at[h], retw_s.at[0], retw_r.at[h], t).wait_recv()
+            to_inner(
+                ret.at[0, pl.ds(64, 32)], back.at[h, pl.ds(64, 32)], rq_s.at[0], rq_r.at[h], t
+            ).wait_recv()
+            to_inner(
+                ret.at[0, pl.ds(0, 64)], back.at[h, pl.ds(0, 64)], rk_s.at[0], rk_r.at[h], t
+            ).wait_recv()
+            to_inner(retw.at[0], back.at[h, pl.ds(96, 16)], rw_s.at[0], rw_r.at[h], t).wait_recv()
+            to_inner(msg_w.at[h], rx_w.at[inner], mw_s.at[h], mw_r.at[inner], t).wait_send()
+            to_inner(msg_k.at[h], rx_k.at[inner], mk_s.at[h], mk_r.at[inner], t).wait_send()
+            to_inner(msg_q.at[h], rx_q.at[inner], mq_s.at[h], mq_r.at[inner], t).wait_send()
+            to_inner(st_tx.at[h // 2], st_rx.at[inner], st_s.at[h], st_r.at[inner], t).wait_send()
 
         return 0
 
-    lax.fori_loop(0, HEADS, get_ret, 0)
-
-    def finish(p, _):
-        cols = pl.ds(pl.multiple_of(p * 128, 128), 128)
-        kvs, qs, rest = [], [], []
-        for a in range(2):
-            h = 2 * p + a
-            om, ow = om_ref[h], ow_ref[h]
-            r = iota((1, 112), 1)
-            t = iota((T, 112), 0)
-            back = jnp.concatenate([ret_rx[h], retw_rx[h]], axis=0)
-            want_kv = jnp.where(r < 64, 4 * r + om, jnp.where((r >= 96) & (r < 100), 64 * (r - 96) + ow, -1))
-            in_q = (r >= 64) & (r < 96)
-            want_q = jnp.where(
-                in_q, 4 * (r - 64) + om, jnp.where((r >= 100) & (r < 104), 64 * (r - 100) + ow, -1)
-            )
-            want_r = jnp.where(in_q, 4 * (r - 32) + om, -1)
-            kvs.append(acc_kv[h] + nn(onehot(t == want_kv), back))
-            qs.append(acc_q[h] + nn(onehot(t == want_q), back))
-            rest.append(nn(onehot(t == want_r), back))
-        dq = jnp.where(left, qs[0] + swap(rest[0]), swap(qs[1]) + rest[1])
-        dq_ref[:, cols] = (SCALE * dq).astype(BF)
-        dk_ref[:, cols] = (SCALE * jnp.where(left, kvs[0], swap(kvs[1]))).astype(BF)
-        dv_ref[:, cols] = jnp.where(left, swap(kvs[0]), kvs[1]).astype(BF)
-        return 0
-
-    lax.fori_loop(0, HEADS // 2, finish, 0)
-
-    def sent_heads(h, _):
-        t = device_of(h)
-
-        @pl.when(t != inner)
-        def _():
-            to_inner(msg.at[h], rx.at[inner], msg_s.at[h], msg_r.at[inner], t).wait_send()
-            to_inner(st_tx.at[h // 2], st_rx.at[inner], st_s.at[h], st_r.at[inner], t).wait_send()
-
-        return 0
-
-    lax.fori_loop(0, HEADS, sent_heads, 0)
+    lax.fori_loop(0, HEADS, get_back, 0)
 
     @pl.when(active)
     def _():
         def sent(d, _):
             t = (inner + d) % N
             to_inner(ls_tx.at[t // 2], ls_rx.at[head], ls_s.at[t], ls_r.at[head], t).wait_send()
-            to_inner(ret.at[t], ret_rx.at[head], ret_s.at[t], ret_r.at[head], t).wait_send()
-            to_inner(retw.at[t], retw_rx.at[head], retw_s.at[t], retw_r.at[head], t).wait_send()
+            to_inner(
+                ret.at[t, pl.ds(64, 32)], back.at[head, pl.ds(64, 32)], rq_s.at[t], rq_r.at[head], t
+            ).wait_send()
+            to_inner(
+                ret.at[t, pl.ds(0, 64)], back.at[head, pl.ds(0, 64)], rk_s.at[t], rk_r.at[head], t
+            ).wait_send()
+            to_inner(retw.at[t], back.at[head, pl.ds(96, 16)], rw_s.at[t], rw_r.at[head], t).wait_send()
             t = (outer + d) % N
             to_outer(yw, rxo.at[outer], yw_s.at[t], yw_r.at[outer], t).wait_send()
             to_outer(wp.at[t], rxp.at[outer], wp_s.at[t], wp_r.at[outer], t).wait_send()
@@ -539,22 +567,63 @@
         lax.fori_loop(1, N, sent, 0)
 
 
+def finish(acc_kv, acc_q, back, where_back, dq_hbm, dk_hbm, dv_hbm, dq_ref, dk_ref, dv_ref, sems):
+    left = iota((1, 128), 1) < 64
+    copies = []
+    for p in range(HEADS // 2):
+        cols = pl.ds(p * 128, 128)
+        kvs, qs, rest = [], [], []
+        for a in range(2):
+            h = 2 * p + a
+            rows = back[h]
+            kvs.append(acc_kv[h] + nn(where_back[h, 0], rows))
+            qs.append(acc_q[h] + nn(where_back[h, 1], rows))
+            rest.append(nn(where_back[h, 2], rows))
+        dq = jnp.where(left, qs[0] + swap(rest[0]), swap(qs[1]) + rest[1])
+        dq_ref[:, cols] = (SCALE * dq).astype(BF)
+        dk_ref[:, cols] = (SCALE * jnp.where(left, kvs[0], swap(kvs[1]))).astype(BF)
+        dv_ref[:, cols] = jnp.where(left, swap(kvs[0]), kvs[1]).astype(BF)
+        if p % 2 == 1:
+            wide = pl.ds((p - 1) * 128, 256)
+            for i, (src, dst) in enumerate([(dq_ref, dq_hbm), (dk_ref, dk_hbm), (dv_ref, dv_hbm)]):
+                copies.append(pltpu.make_async_copy(src.at[:, wide], dst.at[:, wide], sems.at[i, p // 2]))
+                copies[-1].start()
+    for copy in copies:
+        copy.wait()
+
+
 def per_device(queries, keys, values, saved_out, out_grad, offset_mid, offset_wide):
-    out = jax.ShapeDtypeStruct((T, HEADS * 64), BF)
     vmem = pl.BlockSpec(memory_space=pltpu.VMEM)
-    smem = pl.BlockSpec(memory_space=pltpu.SMEM)
+    hbm = pl.BlockSpec(memory_space=pltpu.HBM)
     v = pltpu.VMEM
     dma = pltpu.SemaphoreType.DMA
-    return pl.pallas_call(
+    rows = jax.ShapeDtypeStruct((T, HEADS * 64), BF)
+    parts = pl.pallas_call(
         kernel,
-        out_shape=(out, out, out),
-        in_specs=[smem, smem] + [vmem] * 5,
-        out_specs=(vmem, vmem, vmem),
+        out_shape=(
+            jax.ShapeDtypeStruct((HEADS, T, 128), F32),
+            jax.ShapeDtypeStruct((HEADS, T, 128), F32),
+            jax.ShapeDtypeStruct((HEADS, BACK, 128), BF),
+            jax.ShapeDtypeStruct((HEADS, 3, T, BACK), BF),
+        ),
+        in_specs=[hbm] * 7,
+        out_specs=(vmem,) * 4,
         scratch_shapes=[
+            pltpu.SMEM((HEADS,), I32),
+            pltpu.SMEM((HEADS,), I32),
+            v((T, HEADS * 64), BF),
+            v((T, HEADS * 64), BF),
+            v((T, HEADS * 64), BF),
+            v((T, HEADS * 64), BF),
+            v((T, HEADS * 64), BF),
             v((HEADS, T, 128), BF),
             v((HEADS, T, 128), BF),
-            v((HEADS, MSG, 128), BF),
-            v((N, MSG, 128), BF),
+            v((HEADS, 16, 128), BF),
+            v((HEADS, 64, 128), BF),
+            v((HEADS, 64, 128), BF),
+            v((N, 16, 128), BF),
+            v((N, 64, 128), BF),
+            v((N, 64, 128), BF),
             v((HEADS, T, T), BF),
             v((HEADS, T, T), BF),
             v((HEADS // 2, 8, T), F32),
@@ -570,18 +639,18 @@
             v((8, 128), F32),
             v((8, 128), F32),
             v((8, 128), F32),
+            v((4, T, 128), F32),
             v((N * 64, 128), BF),
             v((64, 128), BF),
             v((64, 128), BF),
             v((N, 64, 128), BF),
             v((N, 64, 128), BF),
             v((N, 64, 128), BF),
-            v((N, RET, 128), BF),
+            v((N, 96, 128), BF),
             v((N, 16, 128), BF),
-            v((HEADS, RET, 128), BF),
-            v((HEADS, 16, 128), BF),
-            v((HEADS, T, 128), F32),
-            v((HEADS, T, 128), F32),
+            dma((7,)),
+            dma((HEADS,)), dma((N,)),
+            dma((HEADS,)), dma((N,)),
             dma((HEADS,)), dma((N,)),
             dma((HEADS,)), dma((N,)),
             dma((N,)), dma((HEADS,)),
@@ -589,11 +658,25 @@
             dma((N,)), dma((N,)),
             dma((N,)), dma((HEADS,)),
             dma((N,)), dma((HEADS,)),
+            dma((N,)), dma((HEADS,)),
         ],
         compiler_params=pltpu.CompilerParams(
-            collective_id=0, has_side_effects=True, vmem_limit_bytes=48 * 1024 * 1024
+            collective_id=0, has_side_effects=True, vmem_limit_bytes=40 * 1024 * 1024
         ),
-    )(offset_mid, offset_wide, queries, keys, values, saved_out, out_grad)
+    )(
+        *[
+            pltpu.with_memory_space_constraint(x, pltpu.HBM)
+            for x in (offset_mid, offset_wide, queries, keys, values, saved_out, out_grad)
+        ]
+    )
+    return pl.pallas_call(
+        finish,
+        out_shape=(rows, rows, rows),
+        in_specs=[vmem] * 4,
+        out_specs=(hbm,) * 3,
+        scratch_shapes=[v((T, HEADS * 64), BF)] * 3 + [dma((3, 3))],
+        compiler_params=pltpu.CompilerParams(vmem_limit_bytes=40 * 1024 * 1024),
+    )(*parts)
 
 
 def solution(mesh):

time: 63.5 us -> 54.6 us (0.86)
  local copies, waits for them, and re-layouts: 8.52 us -> 0 us
    unnamed x17 -> x0, local copies, waits for them, and re-layouts: 8.52 us -> none
    pallas_call x1 -> x2, Pallas kernels: 54 us -> 53.8 us  [the longest x1 52 us: per_device(): pl.pallas_call(kernel, out_shape=(jax.ShapeDtypeStruct((HEADS, T, 128), F...]
where the time goes in v2:
time: 54.6 us; the launch traced here: 54.5 us
  Pallas kernels  53.8 us (99%)
  between operations  0.64 us (1%)
    pallas_call x1, Pallas kernels, per_device(): pl.pallas_call(kernel, out_shape=(jax.ShapeDtypeStruct((HEADS, T, 128), F...  52 us
    pallas_call x1, Pallas kernels, per_device(): pl.pallas_call(finish, out_shape=(rows, rows, rows), in_specs=[vmem] * 4,...  1.8 us

profile of v2, /device:TPU:1, one launch (start us, length us, event | category | flops | bytes accessed | tf_op | source)
XLA Modules:
  0.0 54.5 jit_solution(9282580145857010514)
XLA Ops:
  0.6 52.0 %shard_map.94 = (f32[12,256,128]{2,1,0:T(8,128)S(1)}, f32[12,256,128]{2,1,0:T(8,128)S(1)}, bf16[12,112,128]{2,1,0:T(8,128)(2,1)S(1)}, bf16[12,3,256,112]{3,2,1,0:T(8,128)(2,1)S(1)}) custom-call(s32[12]{0:T(128)} %om_hbm.1, s32[12]{0:T(128)} %ow_hbm.1, bf16[256,768]{1,0:T(8,128)(2,1)} %q_hbm.1, bf16[256,768]{1,0:T(8,128)(2,1)} %k_hbm.1, ...), custom_call_target="tpu_custom_call" | custom-call | tf_op jit(solution)/shard_map/pallas_call | solution.py:601
  52.7 1.8 %shard_map.95 = (bf16[256,768]{1,0:T(8,128)(2,1)}, bf16[256,768]{1,0:T(8,128)(2,1)}, bf16[256,768]{1,0:T(8,128)(2,1)}) custom-call(f32[12,256,128]{2,1,0:T(8,128)S(1)} %get-tuple-element.7.acc_kv, f32[12,256,128]{2,1,0:T(8,128)S(1)} %get-tuple-element.8.acc_q, bf16[12,112,128]{2,1,0:T(8,128)(2,1)S(1)} %get-tuple-element.9.back, ...), custom_call_target="tpu_custom_call" | custom-call | tf_op jit(solution)/shard_map/pallas_call | solution.py:672

commit v3 on v2

v3 whole, which is shorter than its diff:
```python
import jax
import jax.numpy as jnp
from jax import lax
from jax.experimental import pallas as pl
from jax.experimental.pallas import tpu as pltpu
from jax.sharding import PartitionSpec as P

BF = jnp.bfloat16
F32 = jnp.float32
I32 = jnp.int32

N = 16
HEADS = 12
T = 256
MID = 64
SCALE = 0.125
NEG = -1e30
BACK = 112


def iota(shape, dim):
    return lax.broadcasted_iota(I32, shape, dim)


def nn(a, b):
    return lax.dot_general(a, b, (((1,), (0,)), ((), ())), preferred_element_type=F32)


def nt(a, b):
    return lax.dot_general(a, b, (((1,), (1,)), ((), ())), preferred_element_type=F32)


def tn(a, b):
    return lax.dot_general(a, b, (((0,), (0,)), ((), ())), preferred_element_type=F32)


def onehot(mask):
    return jnp.where(mask, 1.0, 0.0).astype(BF)


def split3(x):
    a = x.astype(BF).astype(F32)
    r = x - a
    b = r.astype(BF).astype(F32)
    return jnp.concatenate([a, b, r - b], axis=0).astype(BF)


def sum3(x):
    r = x.shape[0] // 3
    return x[:r] + x[r : 2 * r] + x[2 * r :]


def lse3(a, b, c):
    top = jnp.maximum(a, jnp.maximum(b, c))
    return top + jnp.log(jnp.exp(a - top) + jnp.exp(b - top) + jnp.exp(c - top))


def swap(x):
    return pltpu.roll(x, 64, 1)


def kernel(
    om_hbm, ow_hbm, q_hbm, k_hbm, v_hbm, o_hbm, g_hbm,
    acc_kv, acc_q, back, where_back,
    om_ref, ow_ref, q_ref, k_ref, v_ref, o_ref, g_ref,
    xl, yl, msg_w, msg, rx_w, rx, el, gl, dl, top_l, sum_l, cols_l, st_tx, st_rx, ls_tx, ls_rx,
    yk, yv, s_scr, em, gm, mm, sm, dm, lm, wm, dq_m, xw_all, xw_w, yw, rxo, wp, rxp, ret, retw,
    in_s, mw_s, mw_r, m_s, m_r, st_s, st_r, ls_s, ls_r, yw_s, yw_r, wp_s, wp_r,
    rk_s, rk_r, rq_s, rq_r, rw_s, rw_r,
):
    inner = lax.axis_index("inner")
    outer = lax.axis_index("outer")
    quad = inner // 4
    active = inner % 4 < 3
    head = jnp.minimum(quad * 3 + inner % 4, HEADS - 1)

    def to_inner(src, dst, send, recv, target):
        return pltpu.make_async_remote_copy(
            src_ref=src, dst_ref=dst, send_sem=send, recv_sem=recv,
            device_id={"inner": target}, device_id_type=pl.DeviceIdType.MESH,
        )

    def to_outer(src, dst, send, recv, target):
        return pltpu.make_async_remote_copy(
            src_ref=src, dst_ref=dst, send_sem=send, recv_sem=recv,
            device_id={"outer": target}, device_id_type=pl.DeviceIdType.MESH,
        )

    loads = [
        pltpu.make_async_copy(src, dst, in_s.at[i])
        for i, (src, dst) in enumerate(
            [
                (om_hbm, om_ref), (ow_hbm, ow_ref), (q_hbm, q_ref), (g_hbm, g_ref),
                (k_hbm, k_ref), (v_hbm, v_ref), (o_hbm, o_ref),
            ]
        )
    ]
    for load in loads:
        load.start()

    barrier = pltpu.get_barrier_semaphore()

    def greet(d, _):
        pl.semaphore_signal(
            barrier, inc=1, device_id={"inner": (inner + d) % N}, device_id_type=pl.DeviceIdType.MESH
        )
        pl.semaphore_signal(
            barrier, inc=1, device_id={"outer": (outer + d) % N}, device_id_type=pl.DeviceIdType.MESH
        )
        return 0

    lax.fori_loop(1, N, greet, 0)
    for load in loads:
        load.wait()

    left = iota((1, 128), 1) < 64
    half_k = jnp.where(left, SCALE, 0.0).astype(BF)
    half_v = jnp.where(left, 0.0, 1.0).astype(BF)

    def block_of(u):
        return (quad // 2 + 1 - u // 2) % 2 * 2 + (quad + 1 - u % 2) % 2

    t_row = iota((T, 128), 0)
    t_lane = iota((T, 128), 1)
    place_m = onehot(t_lane == (t_row >> 2) + 64 * (inner % 2))
    place_w = onehot(t_lane == (t_row >> 6) + 4 * inner)
    tok = iota((1, T), 1)
    head_row = iota((16, 1), 0)
    om_col, ow_col = jnp.zeros((16, 1), I32), jnp.zeros((16, 1), I32)
    for h in range(HEADS):
        om_col = jnp.where(head_row == h, om_ref[h], om_col)
        ow_col = jnp.where(head_row == h, ow_ref[h], ow_col)
    keep_m = (tok & 3) == om_col
    keep_w = (tok & 63) == ow_col

    prod = g_ref[...].astype(F32) * o_ref[...].astype(F32)
    hi = prod.astype(BF)
    lo = (prod - hi.astype(F32)).astype(BF)
    of_head = onehot(iota((16, HEADS * 64), 0) == (iota((16, HEADS * 64), 1) >> 6))
    delta = nt(of_head, hi) + nt(of_head, lo)
    dl[...] = delta
    delta_m = nn(split3(jnp.where(keep_m, delta, 0.0)), place_m)
    delta_w = nn(split3(jnp.where(keep_w, delta, 0.0)), place_w)

    row16 = iota((16, 1), 0)
    for p in range(HEADS // 2):
        cols = pl.ds(p * 128, 128)
        qp, kp, vp, gp = q_ref[:, cols], k_ref[:, cols], v_ref[:, cols], g_ref[:, cols]
        for a in range(2):
            h = 2 * p + a
            b, c = 64 * a, 64 * a + 64
            x = jnp.concatenate([qp[:, b:c], gp[:, b:c]], axis=1)
            y = jnp.concatenate([kp[:, b:c], vp[:, b:c]], axis=1)
            xl[h] = x
            yl[h] = y
            om, ow = om_ref[h], ow_ref[h]
            row = iota((96, 1), 0)
            r = row - 64
            w = r & 15
            wide = jnp.where((r < 16) & (w < 4), 64 * w + ow, -1)
            wide = jnp.where((r >= 16) & (w >= 4) & (w < 8), 64 * (w - 4) + ow, wide)
            want = jnp.where(row < 64, 4 * row + om, wide)
            pick = onehot(iota((96, T), 1) == want)
            got = nn(pick, jnp.concatenate([x, y], axis=1))
            msg[h, 0:64, :] = got[0:64, 128:256].astype(BF)
            msg[h, 64:128, :] = got[0:64, 0:128].astype(BF)
            tile = got[64:80, 0:128] + got[80:96, 128:256]
            for i in range(3):
                tile = jnp.where(row16 == 8 + i, delta_m[16 * i + h : 16 * i + h + 1], tile)
                tile = jnp.where(row16 == 11 + i, delta_w[16 * i + h : 16 * i + h + 1], tile)
            msg_w[h] = tile.astype(BF)
    pl.semaphore_wait(barrier, 2 * (N - 1))

    def block_of(u):
        return (quad // 2 + 1 - u // 2) % 2 * 2 + (quad + 1 - u % 2) % 2

    def send_to_heads(src_of, dst, send, recv):
        for i in range(HEADS):
            block = block_of(i // 3)
            j = (i + inner) % 3
            h, target = 3 * block + j, 4 * block + j
            if i < 9:
                to_inner(src_of(h), dst.at[inner], send, recv, target).start()
            else:

                @pl.when(target != inner)
                def _():
                    to_inner(src_of(h), dst.at[inner], send, recv, target).start()

    def got_inner(dst, recv):
        to_inner(dst, dst, recv, recv, (inner + 1) % N).wait_recv()

    def got_outer(dst, recv):
        to_outer(dst, dst, recv, recv, (outer + 1) % N).wait_recv()

    def sent_inner(src, send):
        to_inner(src, src, send, send, (inner + 1) % N).wait_send()

    def sent_outer(src, send):
        to_outer(src, src, send, send, (outer + 1) % N).wait_send()

    send_to_heads(lambda h: msg_w.at[h], rx_w, mw_s, mw_r)
    send_to_heads(lambda h: msg.at[h], rx, m_s, m_r)

    @pl.when(active)
    def _():
        rx_w[inner] = msg_w[head]
        rx[inner] = msg[head]

    top_l[...] = jnp.zeros((16, T), F32)
    sum_l[...] = jnp.ones((16, T), F32)

    def local_a(h, _):
        x, y = xl[h], yl[h]
        s = nt(y * half_k, x)
        top = jnp.max(s, axis=0, keepdims=True)
        e = jnp.exp(s - top)
        top_l[pl.ds(h, 1), :] = top
        sum_l[pl.ds(h, 1), :] = jnp.sum(e, axis=0, keepdims=True)
        d = nt(y * half_v, x)
        el[h] = e.astype(BF)
        gl[h] = (e * (d - dl[pl.ds(h, 1), :])).astype(BF)
        return 0

    lax.fori_loop(0, HEADS, local_a, 0, unroll=3)
    @pl.when(active)
    def _():
        got_inner(rx_w.at[pl.ds(0, N - 1)], mw_r)
        r, c = iota((144, T), 0), iota((144, T), 1)
        slot, owner = c & 15, c >> 4
        at = 16 * ((r & 63) >> 2) + (r & 3)
        j = r - 128
        take = jnp.where(r < 64, jnp.where(c == at, 1, 0), jnp.where(c == at + 4, 1, 0))
        in_m = jnp.where((slot >= 8) & (slot < 11) & ((owner >> 1) == j), 1, 0)
        in_w = jnp.where((slot >= 11) & (slot < 14) & (j == 8), 1, 0)
        take = jnp.where(r < 128, take, in_m + in_w)
        got = nn(onehot(take > 0), rx_w[...].reshape(T, 128))
        xw_w[...] = got[0:64].astype(BF)
        yw[...] = got[64:128].astype(BF)
        dm[...] = got[128:144]
        rxo[outer] = yw[...]
        for d in range(1, N):
            t = (outer + d) % N
            to_outer(yw, rxo.at[outer], yw_s, yw_r, t).start()

    lse_l = top_l[...] + jnp.log(sum_l[...])
    lse_m = sum3(nn(split3(jnp.where(keep_m, lse_l, 0.0)), place_m))
    lse_w = sum3(nn(split3(jnp.where(keep_w, lse_l, 0.0)), place_w))
    row8 = iota((8, 1), 0)
    for h in range(HEADS):
        st_tx[h] = jnp.where(row8 == 0, lse_m[h : h + 1], lse_w[h : h + 1])
    send_to_heads(lambda h: st_tx.at[h], st_rx, st_s, st_r)

    @pl.when(active)
    def _():
        st_rx[inner] = st_tx[head]

    def local_q(h, _):
        acc_q[h] = tn(gl[h], yl[h])
        om, ow = om_ref[h], ow_ref[h]
        r = iota((1, BACK), 1)
        t = iota((T, BACK), 0)
        in_q = (r >= 64) & (r < 96)
        want_kv = jnp.where(r < 64, 4 * r + om, jnp.where((r >= 96) & (r < 100), 64 * (r - 96) + ow, -1))
        want_q = jnp.where(
            in_q, 4 * (r - 64) + om, jnp.where((r >= 100) & (r < 104), 64 * (r - 100) + ow, -1)
        )
        want_r = jnp.where(in_q, 4 * (r - 32) + om, -1)
        where_back[h, 0] = onehot(t == want_kv)
        where_back[h, 1] = onehot(t == want_q)
        where_back[h, 2] = onehot(t == want_r)
        return 0

    lax.fori_loop(0, HEADS, local_q, 0, unroll=3)

    @pl.when(active)
    def _():
        got_inner(rx.at[pl.ds(0, N - 1)], m_r)
        om, ow = om_ref[head], ow_ref[head]
        yk[...] = rx[:, 0:64, :] * half_k
        yv[...] = rx[:, 0:64, :] * half_v

        def mid_a(b):
            x = rx[4 * b : 4 * b + 4, 64:128, :].reshape(T, 128)
            delta = jnp.concatenate([dm[2 * b : 2 * b + 1, :], dm[2 * b + 1 : 2 * b + 2, :]], axis=1)
            top = jnp.full((1, T), NEG, F32)
            for kb in range(4):
                s = nt(yk[4 * kb : 4 * kb + 4].reshape(T, 128), x)
                s_scr[b, kb] = s
                top = jnp.maximum(top, jnp.max(s, axis=0, keepdims=True))
            total = jnp.zeros((1, T), F32)
            dq = jnp.zeros((T, 128), F32)
            for kb in range(4):
                e = jnp.exp(s_scr[b, kb] - top)
                total = total + jnp.sum(e, axis=0, keepdims=True)
                d = nt(yv[4 * kb : 4 * kb + 4].reshape(T, 128), x)
                em[b, kb] = e.astype(BF)
                g = (e * (d - delta)).astype(BF)
                gm[b, kb] = g
                dq = dq + tn(g, rx[4 * kb : 4 * kb + 4, 0:64, :].reshape(T, 128))
            dq_m[b] = dq
            for i in range(2):
                mm[2 * b + i : 2 * b + i + 1, :] = top[:, 128 * i : 128 * i + 128]
                sm[2 * b + i : 2 * b + i + 1, :] = total[:, 128 * i : 128 * i + 128]

        for b in range(4):
            mid_a(b)

        got_inner(st_rx.at[pl.ds(0, N - 1)], st_r)
        ones = onehot(iota((8, N), 0) == (iota((8, N), 1) >> 1))
        rows = st_rx[:, 0, :]
        first = rows.astype(BF).astype(F32)
        second = (rows - first).astype(BF).astype(F32)
        third = rows - first - second
        lm[...] = nn(ones, first.astype(BF)) + nn(ones, second.astype(BF)) + nn(ones, third.astype(BF))
        lse_local_w = jnp.sum(st_rx[:, 1, :], axis=0, keepdims=True)
        got_outer(rxo.at[pl.ds(0, N - 1)], yw_r)

        all_y = rxo[...].reshape(N * 64, 128)
        x_w = xw_w[...]
        s = nt(all_y * half_k, x_w)
        top_w = jnp.max(s, axis=0, keepdims=True)
        e = jnp.exp(s - top_w)
        lse_w = top_w + jnp.log(jnp.sum(e, axis=0, keepdims=True))
        d = nt(all_y * half_v, x_w)
        ew = e.astype(BF)
        gw = (e * (d - dm[8:9, 0:64])).astype(BF)
        s = nt(yk[...].reshape(N * 64, 128), x_w)
        top = jnp.max(s, axis=0, keepdims=True)
        m_at_w = top + jnp.log(jnp.sum(jnp.exp(s - top), axis=0, keepdims=True))
        shared = (ow & 3) == om
        spot = jnp.where(shared, ow >> 2, -1)
        spot_row = jnp.full((1, 64), spot, I32)
        total_w = lse3(lse_w, lse_local_w[:, :64], jnp.where(spot_row >= 0, m_at_w, NEG))
        weight_w = jnp.exp(top_w - total_w)
        zeros64 = jnp.zeros((1, 64), F32)
        col_w = jnp.broadcast_to(jnp.concatenate([weight_w, zeros64], axis=1), (128, 128)).T[0:64, 0:1]
        scaled = (x_w.astype(F32) * col_w).astype(BF)
        wp[...] = jnp.where(left, nn(gw, scaled), nn(ew, scaled)).astype(BF).reshape(N, 64, 128)
        rxp[outer] = wp[outer]

        for d in range(1, N):
            t = (outer + d) % N
            to_outer(wp.at[t], rxp.at[outer], wp_s, wp_r, t).start()

        dq_w = (tn(gw, all_y) * col_w).astype(BF)

        lse_w = jnp.concatenate([lse_w, zeros64], axis=1)
        lane8, chunk8 = iota((8, 128), 1), iota((8, 128), 0)
        n128 = iota((128, 128), 1)
        spread = onehot(((n128 & 7) == (iota((128, 128), 0) >> 4)) & (n128 < 64))
        w_at_m = sum3(nt(split3(jnp.where((lane8 >> 3) == chunk8, lse_w, 0.0)), spread))
        wm[...] = jnp.where((lane8 & 15) == spot, w_at_m, NEG)

        for b in range(4, 4):
            mid_a(b)
        lse_m = mm[...] + jnp.log(sm[...])
        weight_m = jnp.exp(mm[...] - lse3(lse_m, lm[...], wm[...]))
        columns = jnp.concatenate([weight_m, jnp.zeros((120, 128), F32)], axis=0).T
        for j in range(8):
            ls_tx[j] = jnp.where(chunk8 == 0, lse_m[j : j + 1], lse_w)
            col = columns[:, j : j + 1]
            x = rx[2 * j : 2 * j + 2, 64:128, :].reshape(128, 128).astype(F32)
            xw_all[j // 2, 128 * (j % 2) : 128 * (j % 2) + 128, :] = (x * col).astype(BF)
            dq = dq_m[j // 2, 128 * (j % 2) : 128 * (j % 2) + 128, :] * col
            for i in range(2):
                mine = dq[64 * i : 64 * i + 64]
                ret[2 * j + i, 64:96, :] = jnp.where(left, mine[:32], swap(mine[32:])).astype(BF)
        for d in range(1, N):
            t = (inner + d) % N
            to_inner(ls_tx.at[t // 2], ls_rx.at[head], ls_s, ls_r, t).start()
        for d in range(1, N):
            t = (inner + d) % N
            to_inner(ret.at[t, pl.ds(64, 32)], back.at[head, pl.ds(64, 32)], rq_s, rq_r, t).start()
        ls_rx[head] = ls_tx[inner // 2]

        def mid_b(u, _):
            kb = block_of(u)
            from_g = jnp.zeros((T, 128), F32)
            from_e = jnp.zeros((T, 128), F32)
            for b in range(4):
                x = xw_all[b]
                from_g = from_g + nn(gm[b, kb], x)
                from_e = from_e + nn(em[b, kb], x)
            both = jnp.where(left, from_g, from_e).astype(BF)
            ret[pl.ds(4 * kb, 4), 0:64, :] = both.reshape(4, 64, 128)

            for j in range(4):
                t = 4 * kb + (inner + j) % 4

                @pl.when(t != inner)
                def _():
                    to_inner(ret.at[t, pl.ds(0, 64)], back.at[head, pl.ds(0, 64)], rk_s, rk_r, t).start()

            return 0

        lax.fori_loop(0, 4, mid_b, 0)
        back[head, 0:96, :] = ret[inner]

        got_outer(rxp.at[pl.ds(0, N - 1)], wp_r)
        kv_w = jnp.sum(rxp[...].astype(F32), axis=0).astype(BF)
        r256, n64 = iota((T, 64), 0), iota((T, 64), 1)
        slot = r256 & 15
        at = 4 * (r256 >> 4) + (slot & 3)
        rows_w = nn(onehot((n64 == at) & (slot < 4)), kv_w)
        rows_w = rows_w + nn(onehot((n64 == at) & (slot >= 4) & (slot < 8)), dq_w)
        retw[...] = rows_w.astype(BF).reshape(N, 16, 128)

        for d in range(1, N):
            t = (inner + d) % N
            to_inner(retw.at[t], back.at[head, pl.ds(96, 16)], rw_s, rw_r, t).start()
        back[head, 96:112, :] = retw[inner]

    @pl.when(active)
    def _():
        got_inner(ls_rx.at[pl.ds(0, HEADS - 1)], ls_r)

    @pl.when(jnp.logical_not(active))
    def _():
        got_inner(ls_rx, ls_r)

    pad = jnp.zeros((4, 128), F32)
    lse_m = sum3(nt(split3(jnp.concatenate([ls_rx[:, 0, :], pad], axis=0)), place_m))
    lse_w = sum3(nt(split3(jnp.concatenate([ls_rx[:, 1, :], pad], axis=0)), place_w))
    total = lse3(lse_l, jnp.where(keep_m, lse_m, NEG), jnp.where(keep_w, lse_w, NEG))
    weight = jnp.exp(top_l[...] - total)
    cols_l[...] = jnp.concatenate([weight, jnp.zeros((112, T), F32)], axis=0).T
    for h in range(HEADS):
        col = cols_l[:, h : h + 1]
        x = (xl[h].astype(F32) * col).astype(BF)
        acc_kv[h] = jnp.where(left, nn(gl[h], x), nn(el[h], x))
        acc_q[h] = acc_q[h] * col

    def close(heads):
        got_inner(back.at[pl.ds(0, heads), pl.ds(64, 32)], rq_r)
        got_inner(back.at[pl.ds(0, heads), pl.ds(0, 64)], rk_r)
        got_inner(back.at[pl.ds(0, heads), pl.ds(96, 16)], rw_r)
        sent_inner(msg_w.at[pl.ds(0, heads)], mw_s)
        sent_inner(msg.at[pl.ds(0, heads)], m_s)
        sent_inner(st_rx.at[pl.ds(0, heads)], st_s)

    @pl.when(active)
    def _():
        close(HEADS - 1)
        sent_inner(st_rx.at[pl.ds(0, N - 1)], ls_s)
        sent_inner(ret.at[pl.ds(0, N - 1), pl.ds(64, 32)], rq_s)
        sent_inner(ret.at[pl.ds(0, N - 1), pl.ds(0, 64)], rk_s)
        sent_inner(retw.at[pl.ds(0, N - 1)], rw_s)
        sent_outer(rxo.at[pl.ds(0, N - 1)], yw_s)
        sent_outer(wp.at[pl.ds(0, N - 1)], wp_s)

    @pl.when(jnp.logical_not(active))
    def _():
        close(HEADS)


def finish(acc_kv, acc_q, back, where_back, dq_hbm, dk_hbm, dv_hbm, dq_ref, dk_ref, dv_ref, sems):
    left = iota((1, 128), 1) < 64
    copies = []
    for p in range(HEADS // 2):
        cols = pl.ds(p * 128, 128)
        kvs, qs, rest = [], [], []
        for a in range(2):
            h = 2 * p + a
            rows = back[h]
            kvs.append(acc_kv[h] + nn(where_back[h, 0], rows))
            qs.append(acc_q[h] + nn(where_back[h, 1], rows))
            rest.append(nn(where_back[h, 2], rows))
        dq = jnp.where(left, qs[0] + swap(rest[0]), swap(qs[1]) + rest[1])
        dq_ref[:, cols] = (SCALE * dq).astype(BF)
        dk_ref[:, cols] = (SCALE * jnp.where(left, kvs[0], swap(kvs[1]))).astype(BF)
        dv_ref[:, cols] = jnp.where(left, swap(kvs[0]), kvs[1]).astype(BF)
        if p % 2 == 1:
            wide = pl.ds((p - 1) * 128, 256)
            for i, (src, dst) in enumerate([(dq_ref, dq_hbm), (dk_ref, dk_hbm), (dv_ref, dv_hbm)]):
                copies.append(pltpu.make_async_copy(src.at[:, wide], dst.at[:, wide], sems.at[i, p // 2]))
                copies[-1].start()
    for copy in copies:
        copy.wait()


def per_device(queries, keys, values, saved_out, out_grad, offset_mid, offset_wide):
    vmem = pl.BlockSpec(memory_space=pltpu.VMEM)
    hbm = pl.BlockSpec(memory_space=pltpu.HBM)
    v = pltpu.VMEM
    dma = pltpu.SemaphoreType.DMA
    rows = jax.ShapeDtypeStruct((T, HEADS * 64), BF)
    parts = pl.pallas_call(
        kernel,
        out_shape=(
            jax.ShapeDtypeStruct((HEADS, T, 128), F32),
            jax.ShapeDtypeStruct((HEADS, T, 128), F32),
            jax.ShapeDtypeStruct((HEADS, BACK, 128), BF),
            jax.ShapeDtypeStruct((HEADS, 3, T, BACK), BF),
        ),
        in_specs=[hbm] * 7,
        out_specs=(vmem,) * 4,
        scratch_shapes=[
            pltpu.SMEM((HEADS,), I32),
            pltpu.SMEM((HEADS,), I32),
            v((T, HEADS * 64), BF),
            v((T, HEADS * 64), BF),
            v((T, HEADS * 64), BF),
            v((T, HEADS * 64), BF),
            v((T, HEADS * 64), BF),
            v((HEADS, T, 128), BF),
            v((HEADS, T, 128), BF),
            v((HEADS, 16, 128), BF),
            v((HEADS, 128, 128), BF),
            v((N, 16, 128), BF),
            v((N, 128, 128), BF),
            v((HEADS, T, T), BF),
            v((HEADS, T, T), BF),
            v((16, T), F32),
            v((16, T), F32),
            v((16, T), F32),
            v((T, 128), F32),
            v((HEADS, 8, 128), F32),
            v((N, 8, 128), F32),
            v((8, 8, 128), F32),
            v((HEADS, 8, 128), F32),
            v((N, 64, 128), BF),
            v((N, 64, 128), BF),
            v((4, 4, T, T), F32),
            v((4, 4, T, T), BF),
            v((4, 4, T, T), BF),
            v((8, 128), F32),
            v((8, 128), F32),
            v((16, 128), F32),
            v((8, 128), F32),
            v((8, 128), F32),
            v((4, T, 128), F32),
            v((4, T, 128), BF),
            v((64, 128), BF),
            v((64, 128), BF),
            v((N, 64, 128), BF),
            v((N, 64, 128), BF),
            v((N, 64, 128), BF),
            v((N, 96, 128), BF),
            v((N, 16, 128), BF),
            dma((7,)),
            dma, dma,
            dma, dma,
            dma, dma,
            dma, dma,
            dma, dma,
            dma, dma,
            dma, dma,
            dma, dma,
            dma, dma,
        ],
        compiler_params=pltpu.CompilerParams(
            collective_id=0, has_side_effects=True, vmem_limit_bytes=44 * 1024 * 1024
        ),
    )(
        *[
            pltpu.with_memory_space_constraint(x, pltpu.HBM)
            for x in (offset_mid, offset_wide, queries, keys, values, saved_out, out_grad)
        ]
    )
    return pl.pallas_call(
        finish,
        out_shape=(rows, rows, rows),
        in_specs=[vmem] * 4,
        out_specs=(hbm,) * 3,
        scratch_shapes=[v((T, HEADS * 64), BF)] * 3 + [dma((3, 3))],
        compiler_params=pltpu.CompilerParams(vmem_limit_bytes=40 * 1024 * 1024),
    )(*parts)


def solution(mesh):
    rows = P(("outer", "inner"), None)
    return jax.shard_map(
        per_device,
        mesh=mesh,
        in_specs=(rows, rows, rows, rows, rows, P(), P()),
        out_specs=(rows, rows, rows),
        check_vma=False,
    )
```

time: 54.6 us -> 48.7 us (0.89)
  Pallas kernels: 53.8 us -> 47.9 us
    pallas_call x1, Pallas kernels: 52 us -> 46.1 us  [per_device(): pl.pallas_call(kernel, out_shape=(jax.ShapeDtypeStruct((HEADS, T, 128), F...]
where the time goes in v3:
time: 48.7 us; the launch traced here: 48.6 us
  Pallas kernels  47.9 us (98%)
  between operations  0.64 us (1%)
    pallas_call x1, Pallas kernels, per_device(): pl.pallas_call(kernel, out_shape=(jax.ShapeDtypeStruct((HEADS, T, 128), F...  46.1 us
    pallas_call x1, Pallas kernels, per_device(): pl.pallas_call(finish, out_shape=(rows, rows, rows), in_specs=[vmem] * 4,...  1.8 us

profile of v3, /device:TPU:1, one launch (start us, length us, event | category | flops | bytes accessed | tf_op | source)
XLA Modules:
  0.0 48.6 jit_solution(1297625590368437973)
XLA Ops:
  0.6 46.1 %shard_map.94 = (f32[12,256,128]{2,1,0:T(8,128)S(1)}, f32[12,256,128]{2,1,0:T(8,128)S(1)}, bf16[12,112,128]{2,1,0:T(8,128)(2,1)S(1)}, bf16[12,3,256,112]{3,2,1,0:T(8,128)(2,1)S(1)}) custom-call(s32[12]{0:T(128)} %om_hbm.1, s32[12]{0:T(128)} %ow_hbm.1, bf16[256,768]{1,0:T(8,128)(2,1)} %q_hbm.1, bf16[256,768]{1,0:T(8,128)(2,1)} %k_hbm.1, ...), custom_call_target="tpu_custom_call" | custom-call | tf_op jit(solution)/shard_map/pallas_call | solution.py:488
  46.8 1.8 %shard_map.95 = (bf16[256,768]{1,0:T(8,128)(2,1)}, bf16[256,768]{1,0:T(8,128)(2,1)}, bf16[256,768]{1,0:T(8,128)(2,1)}) custom-call(f32[12,256,128]{2,1,0:T(8,128)S(1)} %get-tuple-element.7.acc_kv, f32[12,256,128]{2,1,0:T(8,128)S(1)} %get-tuple-element.8.acc_q, bf16[12,112,128]{2,1,0:T(8,128)(2,1)S(1)} %get-tuple-element.9.back, ...), custom_call_target="tpu_custom_call" | custom-call | tf_op jit(solution)/shard_map/pallas_call | solution.py:561

commit v4 on v3

--- a/solution.py
+++ b/solution.py
@@ -64,8 +64,8 @@
     acc_kv, acc_q, back, where_back,
     om_ref, ow_ref, q_ref, k_ref, v_ref, o_ref, g_ref,
     xl, yl, msg_w, msg, rx_w, rx, el, gl, dl, top_l, sum_l, cols_l, st_tx, st_rx, ls_tx, ls_rx,
-    yk, yv, s_scr, em, gm, mm, sm, dm, lm, wm, dq_m, xw_all, xw_w, yw, rxo, wp, rxp, ret, retw,
-    in_s, mw_s, mw_r, m_s, m_r, st_s, st_r, ls_s, ls_r, yw_s, yw_r, wp_s, wp_r,
+    yk, yv, s_scr, em, gm, mm, sm, dm, lm, wm, xw_all, xw_w, yw, rxo, wp, rxp, ret, retw,
+    in_s, mw_s, mw_r, mk_s, mk_r, mq_s, mq_r, st_s, st_r, ls_s, ls_r, yw_s, yw_r, wp_s, wp_r,
     rk_s, rk_r, rq_s, rq_r, rw_s, rw_r,
 ):
     inner = lax.axis_index("inner")
@@ -95,10 +95,10 @@
             ]
         )
     ]
+    barrier = pltpu.get_barrier_semaphore()
+
     for load in loads:
         load.start()
-
-    barrier = pltpu.get_barrier_semaphore()
 
     def greet(d, _):
         pl.semaphore_signal(
@@ -174,18 +174,19 @@
     def block_of(u):
         return (quad // 2 + 1 - u // 2) % 2 * 2 + (quad + 1 - u % 2) % 2
 
-    def send_to_heads(src_of, dst, send, recv):
+    def send_to_heads(src_of, dst, send, recv, rows=None):
+        place = dst.at[inner] if rows is None else dst.at[inner, rows]
         for i in range(HEADS):
             block = block_of(i // 3)
             j = (i + inner) % 3
             h, target = 3 * block + j, 4 * block + j
             if i < 9:
-                to_inner(src_of(h), dst.at[inner], send, recv, target).start()
+                to_inner(src_of(h), place, send, recv, target).start()
             else:
 
                 @pl.when(target != inner)
                 def _():
-                    to_inner(src_of(h), dst.at[inner], send, recv, target).start()
+                    to_inner(src_of(h), place, send, recv, target).start()
 
     def got_inner(dst, recv):
         to_inner(dst, dst, recv, recv, (inner + 1) % N).wait_recv()
@@ -200,7 +201,8 @@
         to_outer(src, src, send, send, (outer + 1) % N).wait_send()
 
     send_to_heads(lambda h: msg_w.at[h], rx_w, mw_s, mw_r)
-    send_to_heads(lambda h: msg.at[h], rx, m_s, m_r)
+    send_to_heads(lambda h: msg.at[h, pl.ds(0, 64)], rx, mk_s, mk_r, pl.ds(0, 64))
+    send_to_heads(lambda h: msg.at[h, pl.ds(64, 64)], rx, mq_s, mq_r.at[quad], pl.ds(64, 64))
 
     @pl.when(active)
     def _():
@@ -259,52 +261,51 @@
         acc_q[h] = tn(gl[h], yl[h])
         om, ow = om_ref[h], ow_ref[h]
         r = iota((1, BACK), 1)
-        t = iota((T, BACK), 0)
-        in_q = (r >= 64) & (r < 96)
-        want_kv = jnp.where(r < 64, 4 * r + om, jnp.where((r >= 96) & (r < 100), 64 * (r - 96) + ow, -1))
-        want_q = jnp.where(
-            in_q, 4 * (r - 64) + om, jnp.where((r >= 100) & (r < 104), 64 * (r - 100) + ow, -1)
-        )
-        want_r = jnp.where(in_q, 4 * (r - 32) + om, -1)
-        where_back[h, 0] = onehot(t == want_kv)
-        where_back[h, 1] = onehot(t == want_q)
-        where_back[h, 2] = onehot(t == want_r)
+        want = jnp.where(r < 64, 4 * r + om, jnp.where((r >= 96) & (r < 100), 64 * (r - 96) + ow, -1))
+        where_back[h, 0] = onehot(iota((T, BACK), 0) == want)
         return 0
 
     lax.fori_loop(0, HEADS, local_q, 0, unroll=3)
 
     @pl.when(active)
     def _():
-        got_inner(rx.at[pl.ds(0, N - 1)], m_r)
+        got_inner(rx.at[pl.ds(0, N - 1), pl.ds(0, 64)], mk_r)
         om, ow = om_ref[head], ow_ref[head]
         yk[...] = rx[:, 0:64, :] * half_k
         yv[...] = rx[:, 0:64, :] * half_v
 
-        def mid_a(b):
-            x = rx[4 * b : 4 * b + 4, 64:128, :].reshape(T, 128)
-            delta = jnp.concatenate([dm[2 * b : 2 * b + 1, :], dm[2 * b + 1 : 2 * b + 2, :]], axis=1)
+        def mid_a(u):
+            b = block_of(3 - u)
+            got_inner(rx.at[pl.ds(0, 3 if u == 0 else 4), pl.ds(64, 64)], mq_r.at[b])
+            x = rx[pl.ds(4 * b, 4), 64:128, :].reshape(T, 128)
+            delta = jnp.concatenate([dm[pl.ds(2 * b, 1), :], dm[pl.ds(2 * b + 1, 1), :]], axis=1)
             top = jnp.full((1, T), NEG, F32)
             for kb in range(4):
                 s = nt(yk[4 * kb : 4 * kb + 4].reshape(T, 128), x)
-                s_scr[b, kb] = s
+                s_scr[u, kb] = s
                 top = jnp.maximum(top, jnp.max(s, axis=0, keepdims=True))
             total = jnp.zeros((1, T), F32)
             dq = jnp.zeros((T, 128), F32)
             for kb in range(4):
-                e = jnp.exp(s_scr[b, kb] - top)
+                e = jnp.exp(s_scr[u, kb] - top)
                 total = total + jnp.sum(e, axis=0, keepdims=True)
                 d = nt(yv[4 * kb : 4 * kb + 4].reshape(T, 128), x)
                 em[b, kb] = e.astype(BF)
                 g = (e * (d - delta)).astype(BF)
                 gm[b, kb] = g
                 dq = dq + tn(g, rx[4 * kb : 4 * kb + 4, 0:64, :].reshape(T, 128))
-            dq_m[b] = dq
+            for i in range(4):
+                mine = dq[64 * i : 64 * i + 64]
+                ret[4 * b + i, 64:96, :] = jnp.where(left, mine[:32], swap(mine[32:])).astype(BF)
             for i in range(2):
-                mm[2 * b + i : 2 * b + i + 1, :] = top[:, 128 * i : 128 * i + 128]
-                sm[2 * b + i : 2 * b + i + 1, :] = total[:, 128 * i : 128 * i + 128]
-
-        for b in range(4):
-            mid_a(b)
+                mm[pl.ds(2 * b + i, 1), :] = top[:, 128 * i : 128 * i + 128]
+                sm[pl.ds(2 * b + i, 1), :] = total[:, 128 * i : 128 * i + 128]
+            for i in range(1 if u == 0 else 0, 4):
+                t = 4 * b + (inner + i) % 4
+                to_inner(ret.at[t, pl.ds(64, 32)], back.at[head, pl.ds(64, 32)], rq_s, rq_r, t).start()
+
+        for u in range(4):
+            mid_a(u)
 
         got_inner(st_rx.at[pl.ds(0, N - 1)], st_r)
         ones = onehot(iota((8, N), 0) == (iota((8, N), 1) >> 1))
@@ -352,26 +353,17 @@
         w_at_m = sum3(nt(split3(jnp.where((lane8 >> 3) == chunk8, lse_w, 0.0)), spread))
         wm[...] = jnp.where((lane8 & 15) == spot, w_at_m, NEG)
 
-        for b in range(4, 4):
-            mid_a(b)
         lse_m = mm[...] + jnp.log(sm[...])
         weight_m = jnp.exp(mm[...] - lse3(lse_m, lm[...], wm[...]))
         columns = jnp.concatenate([weight_m, jnp.zeros((120, 128), F32)], axis=0).T
         for j in range(8):
-            ls_tx[j] = jnp.where(chunk8 == 0, lse_m[j : j + 1], lse_w)
+            ls_tx[j] = jnp.where(chunk8 == 0, lse_m[j : j + 1], jnp.where(chunk8 == 1, lse_w, mm[j : j + 1, :]))
             col = columns[:, j : j + 1]
             x = rx[2 * j : 2 * j + 2, 64:128, :].reshape(128, 128).astype(F32)
             xw_all[j // 2, 128 * (j % 2) : 128 * (j % 2) + 128, :] = (x * col).astype(BF)
-            dq = dq_m[j // 2, 128 * (j % 2) : 128 * (j % 2) + 128, :] * col
-            for i in range(2):
-                mine = dq[64 * i : 64 * i + 64]
-                ret[2 * j + i, 64:96, :] = jnp.where(left, mine[:32], swap(mine[32:])).astype(BF)
         for d in range(1, N):
             t = (inner + d) % N
             to_inner(ls_tx.at[t // 2], ls_rx.at[head], ls_s, ls_r, t).start()
-        for d in range(1, N):
-            t = (inner + d) % N
-            to_inner(ret.at[t, pl.ds(64, 32)], back.at[head, pl.ds(64, 32)], rq_s, rq_r, t).start()
         ls_rx[head] = ls_tx[inner // 2]
 
         def mid_b(u, _):
@@ -424,19 +416,33 @@
     lse_w = sum3(nt(split3(jnp.concatenate([ls_rx[:, 1, :], pad], axis=0)), place_w))
     total = lse3(lse_l, jnp.where(keep_m, lse_m, NEG), jnp.where(keep_w, lse_w, NEG))
     weight = jnp.exp(top_l[...] - total)
-    cols_l[...] = jnp.concatenate([weight, jnp.zeros((112, T), F32)], axis=0).T
+    top_m = sum3(nt(split3(jnp.concatenate([ls_rx[:, 2, :], pad], axis=0)), place_m))
+    weight_m = jnp.where(keep_m, jnp.exp(jnp.where(keep_m, top_m, NEG) - total), 0.0)
+    cols_l[...] = jnp.concatenate([weight, weight_m, jnp.zeros((96, T), F32)], axis=0).T
     for h in range(HEADS):
         col = cols_l[:, h : h + 1]
         x = (xl[h].astype(F32) * col).astype(BF)
         acc_kv[h] = jnp.where(left, nn(gl[h], x), nn(el[h], x))
         acc_q[h] = acc_q[h] * col
+        col = cols_l[:, 16 + h : 17 + h]
+        r = iota((1, BACK), 1)
+        t = iota((T, BACK), 0)
+        in_q = (r >= 64) & (r < 96)
+        om, ow = om_ref[h], ow_ref[h]
+        want_q = jnp.where(
+            in_q, 4 * (r - 64) + om, jnp.where((r >= 100) & (r < 104), 64 * (r - 100) + ow, -1)
+        )
+        want_r = jnp.where(in_q, 4 * (r - 32) + om, -1)
+        where_back[h, 1] = jnp.where(t == want_q, jnp.where(in_q, col, 1.0), 0.0).astype(BF)
+        where_back[h, 2] = jnp.where(t == want_r, col, 0.0).astype(BF)
 
     def close(heads):
         got_inner(back.at[pl.ds(0, heads), pl.ds(64, 32)], rq_r)
         got_inner(back.at[pl.ds(0, heads), pl.ds(0, 64)], rk_r)
         got_inner(back.at[pl.ds(0, heads), pl.ds(96, 16)], rw_r)
         sent_inner(msg_w.at[pl.ds(0, heads)], mw_s)
-        sent_inner(msg.at[pl.ds(0, heads)], m_s)
+        sent_inner(msg.at[pl.ds(0, heads), pl.ds(0, 64)], mk_s)
+        sent_inner(msg.at[pl.ds(0, heads), pl.ds(64, 64)], mq_s)
         sent_inner(st_rx.at[pl.ds(0, heads)], st_s)
 
     @pl.when(active)
@@ -529,7 +535,6 @@
             v((16, 128), F32),
             v((8, 128), F32),
             v((8, 128), F32),
-            v((4, T, 128), F32),
             v((4, T, 128), BF),
             v((64, 128), BF),
             v((64, 128), BF),
@@ -541,6 +546,7 @@
             dma((7,)),
             dma, dma,
             dma, dma,
+            dma, dma((4,)),
             dma, dma,
             dma, dma,
             dma, dma,

time: 48.7 us -> 47.9 us (0.984)
  Pallas kernels: 47.9 us -> 47.2 us
    pallas_call x1, Pallas kernels: 46.1 us -> 45.4 us  [per_device(): pl.pallas_call(kernel, out_shape=(jax.ShapeDtypeStruct((HEADS, T, 128), F...]
where the time goes in v4:
time: 47.9 us; the launch traced here: 47.8 us
  Pallas kernels  47.2 us (99%)
  between operations  0.64 us (1%)
    pallas_call x1, Pallas kernels, per_device(): pl.pallas_call(kernel, out_shape=(jax.ShapeDtypeStruct((HEADS, T, 128), F...  45.4 us
    pallas_call x1, Pallas kernels, per_device(): pl.pallas_call(finish, out_shape=(rows, rows, rows), in_specs=[vmem] * 4,...  1.8 us

profile of v4, /device:TPU:1, one launch (start us, length us, event | category | flops | bytes accessed | tf_op | source)
XLA Modules:
  0.0 47.8 jit_solution(2434803384487260213)
XLA Ops:
  0.6 45.4 %shard_map.94 = (f32[12,256,128]{2,1,0:T(8,128)S(1)}, f32[12,256,128]{2,1,0:T(8,128)S(1)}, bf16[12,112,128]{2,1,0:T(8,128)(2,1)S(1)}, bf16[12,3,256,112]{3,2,1,0:T(8,128)(2,1)S(1)}) custom-call(s32[12]{0:T(128)} %om_hbm.1, s32[12]{0:T(128)} %ow_hbm.1, bf16[256,768]{1,0:T(8,128)(2,1)} %q_hbm.1, bf16[256,768]{1,0:T(8,128)(2,1)} %k_hbm.1, ...), custom_call_target="tpu_custom_call" | custom-call | tf_op jit(solution)/shard_map/pallas_call | solution.py:494
  46.0 1.8 %shard_map.95 = (bf16[256,768]{1,0:T(8,128)(2,1)}, bf16[256,768]{1,0:T(8,128)(2,1)}, bf16[256,768]{1,0:T(8,128)(2,1)}) custom-call(f32[12,256,128]{2,1,0:T(8,128)S(1)} %get-tuple-element.7.acc_kv, f32[12,256,128]{2,1,0:T(8,128)S(1)} %get-tuple-element.8.acc_q, bf16[12,112,128]{2,1,0:T(8,128)(2,1)S(1)} %get-tuple-element.9.back, ...), custom_call_target="tpu_custom_call" | custom-call | tf_op jit(solution)/shard_map/pallas_call | solution.py:567

commit v5 on v4

--- a/solution.py
+++ b/solution.py
@@ -10,12 +10,13 @@
 I32 = jnp.int32
 
 N = 16
+FAR = (8, 9, 10, 7, 6, 11, 12, 5, 4, 13, 14, 3, 2, 15, 1)
 HEADS = 12
 T = 256
 MID = 64
 SCALE = 0.125
 NEG = -1e30
-BACK = 112
+BACK = 96
 
 
 def iota(shape, dim):
@@ -61,10 +62,10 @@
 
 def kernel(
     om_hbm, ow_hbm, q_hbm, k_hbm, v_hbm, o_hbm, g_hbm,
-    acc_kv, acc_q, back, where_back,
+    fin_q, fin_k, fin_v, back_w, places_w,
     om_ref, ow_ref, q_ref, k_ref, v_ref, o_ref, g_ref,
-    xl, yl, msg_w, msg, rx_w, rx, el, gl, dl, top_l, sum_l, cols_l, st_tx, st_rx, ls_tx, ls_rx,
-    yk, yv, s_scr, em, gm, mm, sm, dm, lm, wm, xw_all, xw_w, yw, rxo, wp, rxp, ret, retw,
+    acc_kv, acc_q, back, where_kv, where_q, xl, yl, msg_w, msg, rx_w, rx, el, gl, dl, top_l, sum_l, cols_l, st_tx, st_rx, ls_tx, ls_rx,
+    yk, yv, s_scr, em, gm, mm, sm, dm, lm, wm, xw_all, xw_w, yw, rxo, wp, rxp, lw, dqw, ret, retw,
     in_s, mw_s, mw_r, mk_s, mk_r, mq_s, mq_r, st_s, st_r, ls_s, ls_r, yw_s, yw_r, wp_s, wp_r,
     rk_s, rk_r, rq_s, rq_r, rw_s, rw_r,
 ):
@@ -119,6 +120,9 @@
 
     def block_of(u):
         return (quad // 2 + 1 - u // 2) % 2 * 2 + (quad + 1 - u % 2) % 2
+
+    def peers():
+        return [4 * block_of(i // 4) + (inner + i) % 4 for i in range(N) if i != 12]
 
     t_row = iota((T, 128), 0)
     t_lane = iota((T, 128), 1)
@@ -241,7 +245,7 @@
         yw[...] = got[64:128].astype(BF)
         dm[...] = got[128:144]
         rxo[outer] = yw[...]
-        for d in range(1, N):
+        for d in FAR:
             t = (outer + d) % N
             to_outer(yw, rxo.at[outer], yw_s, yw_r, t).start()
 
@@ -259,10 +263,7 @@
 
     def local_q(h, _):
         acc_q[h] = tn(gl[h], yl[h])
-        om, ow = om_ref[h], ow_ref[h]
-        r = iota((1, BACK), 1)
-        want = jnp.where(r < 64, 4 * r + om, jnp.where((r >= 96) & (r < 100), 64 * (r - 96) + ow, -1))
-        where_back[h, 0] = onehot(iota((T, BACK), 0) == want)
+        where_kv[h] = onehot(iota((T, 64), 0) == 4 * iota((1, 64), 1) + om_ref[h])
         return 0
 
     lax.fori_loop(0, HEADS, local_q, 0, unroll=3)
@@ -273,6 +274,11 @@
         om, ow = om_ref[head], ow_ref[head]
         yk[...] = rx[:, 0:64, :] * half_k
         yv[...] = rx[:, 0:64, :] * half_v
+
+        x_w = xw_w[...]
+        s = nt(yk[...].reshape(N * 64, 128), x_w)
+        top = jnp.max(s, axis=0, keepdims=True)
+        m_at_w = top + jnp.log(jnp.sum(jnp.exp(s - top), axis=0, keepdims=True))
 
         def mid_a(u):
             b = block_of(3 - u)
@@ -304,65 +310,67 @@
                 t = 4 * b + (inner + i) % 4
                 to_inner(ret.at[t, pl.ds(64, 32)], back.at[head, pl.ds(64, 32)], rq_s, rq_r, t).start()
 
+        lane8, chunk8 = iota((8, 128), 1), iota((8, 128), 0)
+
+        def wide():
+            got_inner(st_rx.at[pl.ds(0, N - 1)], st_r)
+            ones = onehot(iota((8, N), 0) == (iota((8, N), 1) >> 1))
+            rows = st_rx[:, 0, :]
+            first = rows.astype(BF).astype(F32)
+            second = (rows - first).astype(BF).astype(F32)
+            third = rows - first - second
+            lm[...] = nn(ones, first.astype(BF)) + nn(ones, second.astype(BF)) + nn(ones, third.astype(BF))
+            lse_local_w = jnp.sum(st_rx[:, 1, :], axis=0, keepdims=True)
+            got_outer(rxo.at[pl.ds(0, N - 1)], yw_r)
+
+            all_y = rxo[...].reshape(N * 64, 128)
+            s = nt(all_y * half_k, x_w)
+            top_w = jnp.max(s, axis=0, keepdims=True)
+            e = jnp.exp(s - top_w)
+            lse_w = top_w + jnp.log(jnp.sum(e, axis=0, keepdims=True))
+            d = nt(all_y * half_v, x_w)
+            ew = e.astype(BF)
+            gw = (e * (d - dm[8:9, 0:64])).astype(BF)
+            shared = (ow & 3) == om
+            spot = jnp.where(shared, ow >> 2, -1)
+            spot_row = jnp.full((1, 64), spot, I32)
+            total_w = lse3(lse_w, lse_local_w[:, :64], jnp.where(spot_row >= 0, m_at_w, NEG))
+            weight_w = jnp.exp(top_w - total_w)
+            zeros64 = jnp.zeros((1, 64), F32)
+            col_w = jnp.broadcast_to(jnp.concatenate([weight_w, zeros64], axis=1), (128, 128)).T[0:64, 0:1]
+            scaled = (x_w.astype(F32) * col_w).astype(BF)
+            wp[...] = jnp.where(left, nn(gw, scaled), nn(ew, scaled)).astype(BF).reshape(N, 64, 128)
+            rxp[outer] = wp[outer]
+
+            for d in FAR:
+                t = (outer + d) % N
+                to_outer(wp.at[t], rxp.at[outer], wp_s, wp_r, t).start()
+
+            dqw[...] = (tn(gw, all_y) * col_w).astype(BF)
+
+            lse_w = jnp.concatenate([lse_w, zeros64], axis=1)
+            lw[...] = jnp.broadcast_to(lse_w, (8, 128))
+            n128 = iota((128, 128), 1)
+            spread = onehot(((n128 & 7) == (iota((128, 128), 0) >> 4)) & (n128 < 64))
+            w_at_m = sum3(nt(split3(jnp.where((lane8 >> 3) == chunk8, lse_w, 0.0)), spread))
+            wm[...] = jnp.where((lane8 & 15) == spot, w_at_m, NEG)
+
+        late = outer >= 8
         for u in range(4):
+            if u == 3:
+                pl.when(late)(wide)
             mid_a(u)
-
-        got_inner(st_rx.at[pl.ds(0, N - 1)], st_r)
-        ones = onehot(iota((8, N), 0) == (iota((8, N), 1) >> 1))
-        rows = st_rx[:, 0, :]
-        first = rows.astype(BF).astype(F32)
-        second = (rows - first).astype(BF).astype(F32)
-        third = rows - first - second
-        lm[...] = nn(ones, first.astype(BF)) + nn(ones, second.astype(BF)) + nn(ones, third.astype(BF))
-        lse_local_w = jnp.sum(st_rx[:, 1, :], axis=0, keepdims=True)
-        got_outer(rxo.at[pl.ds(0, N - 1)], yw_r)
-
-        all_y = rxo[...].reshape(N * 64, 128)
-        x_w = xw_w[...]
-        s = nt(all_y * half_k, x_w)
-        top_w = jnp.max(s, axis=0, keepdims=True)
-        e = jnp.exp(s - top_w)
-        lse_w = top_w + jnp.log(jnp.sum(e, axis=0, keepdims=True))
-        d = nt(all_y * half_v, x_w)
-        ew = e.astype(BF)
-        gw = (e * (d - dm[8:9, 0:64])).astype(BF)
-        s = nt(yk[...].reshape(N * 64, 128), x_w)
-        top = jnp.max(s, axis=0, keepdims=True)
-        m_at_w = top + jnp.log(jnp.sum(jnp.exp(s - top), axis=0, keepdims=True))
-        shared = (ow & 3) == om
-        spot = jnp.where(shared, ow >> 2, -1)
-        spot_row = jnp.full((1, 64), spot, I32)
-        total_w = lse3(lse_w, lse_local_w[:, :64], jnp.where(spot_row >= 0, m_at_w, NEG))
-        weight_w = jnp.exp(top_w - total_w)
-        zeros64 = jnp.zeros((1, 64), F32)
-        col_w = jnp.broadcast_to(jnp.concatenate([weight_w, zeros64], axis=1), (128, 128)).T[0:64, 0:1]
-        scaled = (x_w.astype(F32) * col_w).astype(BF)
-        wp[...] = jnp.where(left, nn(gw, scaled), nn(ew, scaled)).astype(BF).reshape(N, 64, 128)
-        rxp[outer] = wp[outer]
-
-        for d in range(1, N):
-            t = (outer + d) % N
-            to_outer(wp.at[t], rxp.at[outer], wp_s, wp_r, t).start()
-
-        dq_w = (tn(gw, all_y) * col_w).astype(BF)
-
-        lse_w = jnp.concatenate([lse_w, zeros64], axis=1)
-        lane8, chunk8 = iota((8, 128), 1), iota((8, 128), 0)
-        n128 = iota((128, 128), 1)
-        spread = onehot(((n128 & 7) == (iota((128, 128), 0) >> 4)) & (n128 < 64))
-        w_at_m = sum3(nt(split3(jnp.where((lane8 >> 3) == chunk8, lse_w, 0.0)), spread))
-        wm[...] = jnp.where((lane8 & 15) == spot, w_at_m, NEG)
+        pl.when(jnp.logical_not(late))(wide)
 
         lse_m = mm[...] + jnp.log(sm[...])
         weight_m = jnp.exp(mm[...] - lse3(lse_m, lm[...], wm[...]))
         columns = jnp.concatenate([weight_m, jnp.zeros((120, 128), F32)], axis=0).T
         for j in range(8):
-            ls_tx[j] = jnp.where(chunk8 == 0, lse_m[j : j + 1], jnp.where(chunk8 == 1, lse_w, mm[j : j + 1, :]))
+            ls_tx[j] = jnp.where(chunk8 == 0, lse_m[j : j + 1], jnp.where(chunk8 == 1, lw[...], mm[j : j + 1, :]))
             col = columns[:, j : j + 1]
             x = rx[2 * j : 2 * j + 2, 64:128, :].reshape(128, 128).astype(F32)
             xw_all[j // 2, 128 * (j % 2) : 128 * (j % 2) + 128, :] = (x * col).astype(BF)
-        for d in range(1, N):
-            t = (inner + d) % N
+        for t in peers():
             to_inner(ls_tx.at[t // 2], ls_rx.at[head], ls_s, ls_r, t).start()
         ls_rx[head] = ls_tx[inner // 2]
 
@@ -395,13 +403,12 @@
         slot = r256 & 15
         at = 4 * (r256 >> 4) + (slot & 3)
         rows_w = nn(onehot((n64 == at) & (slot < 4)), kv_w)
-        rows_w = rows_w + nn(onehot((n64 == at) & (slot >= 4) & (slot < 8)), dq_w)
+        rows_w = rows_w + nn(onehot((n64 == at) & (slot >= 4) & (slot < 8)), dqw[...])
         retw[...] = rows_w.astype(BF).reshape(N, 16, 128)
 
-        for d in range(1, N):
-            t = (inner + d) % N
-            to_inner(retw.at[t], back.at[head, pl.ds(96, 16)], rw_s, rw_r, t).start()
-        back[head, 96:112, :] = retw[inner]
+        for t in peers():
+            to_inner(retw.at[t], back_w.at[head], rw_s, rw_r, t).start()
+        back_w[head] = retw[inner]
 
     @pl.when(active)
     def _():
@@ -425,21 +432,43 @@
         acc_kv[h] = jnp.where(left, nn(gl[h], x), nn(el[h], x))
         acc_q[h] = acc_q[h] * col
         col = cols_l[:, 16 + h : 17 + h]
-        r = iota((1, BACK), 1)
-        t = iota((T, BACK), 0)
-        in_q = (r >= 64) & (r < 96)
-        om, ow = om_ref[h], ow_ref[h]
-        want_q = jnp.where(
-            in_q, 4 * (r - 64) + om, jnp.where((r >= 100) & (r < 104), 64 * (r - 100) + ow, -1)
-        )
-        want_r = jnp.where(in_q, 4 * (r - 32) + om, -1)
-        where_back[h, 1] = jnp.where(t == want_q, jnp.where(in_q, col, 1.0), 0.0).astype(BF)
-        where_back[h, 2] = jnp.where(t == want_r, col, 0.0).astype(BF)
+        r = iota((1, 32), 1)
+        t = iota((T, 32), 0)
+        where_q[h, 0] = jnp.where(t == 4 * r + om_ref[h], col, 0.0).astype(BF)
+        where_q[h, 1] = jnp.where(t == 4 * (r + 32) + om_ref[h], col, 0.0).astype(BF)
+
+    c = iota((1, 192), 1)
+    ow_c = jnp.zeros((1, 192), I32)
+    for h in range(HEADS):
+        ow_c = jnp.where((c >> 4) == h, ow_ref[h], ow_c)
+    r = c & 15
+    t = iota((T, 192), 0)
+    places_w[0:T, :] = onehot(t == jnp.where(r < 4, 64 * r + ow_c, -1))
+    places_w[T:, :] = onehot(t == jnp.where((r >= 4) & (r < 8), 64 * (r - 4) + ow_c, -1))
+
+    @pl.when(active)
+    def _():
+        got_inner(back.at[pl.ds(0, HEADS - 1), pl.ds(64, 32)], rq_r)
+        got_inner(back.at[pl.ds(0, HEADS - 1), pl.ds(0, 64)], rk_r)
+
+    @pl.when(jnp.logical_not(active))
+    def _():
+        got_inner(back.at[pl.ds(0, HEADS), pl.ds(64, 32)], rq_r)
+        got_inner(back.at[pl.ds(0, HEADS), pl.ds(0, 64)], rk_r)
+
+    for p in range(HEADS // 2):
+        cols = pl.ds(p * 128, 128)
+        kvs, qs, rest = [], [], []
+        for h in (2 * p, 2 * p + 1):
+            kvs.append(acc_kv[h] + nn(where_kv[h], back[h, 0:64, :]))
+            qs.append(acc_q[h] + nn(where_q[h, 0], back[h, 64:96, :]))
+            rest.append(nn(where_q[h, 1], back[h, 64:96, :]))
+        fin_q[:, cols] = jnp.where(left, qs[0] + swap(rest[0]), swap(qs[1]) + rest[1])
+        fin_k[:, cols] = jnp.where(left, kvs[0], swap(kvs[1]))
+        fin_v[:, cols] = jnp.where(left, swap(kvs[0]), kvs[1])
 
     def close(heads):
-        got_inner(back.at[pl.ds(0, heads), pl.ds(64, 32)], rq_r)
-        got_inner(back.at[pl.ds(0, heads), pl.ds(0, 64)], rk_r)
-        got_inner(back.at[pl.ds(0, heads), pl.ds(96, 16)], rw_r)
+        got_inner(back_w.at[pl.ds(0, heads)], rw_r)
         sent_inner(msg_w.at[pl.ds(0, heads)], mw_s)
         sent_inner(msg.at[pl.ds(0, heads), pl.ds(0, 64)], mk_s)
         sent_inner(msg.at[pl.ds(0, heads), pl.ds(64, 64)], mq_s)
@@ -460,27 +489,27 @@
         close(HEADS)
 
 
-def finish(acc_kv, acc_q, back, where_back, dq_hbm, dk_hbm, dv_hbm, dq_ref, dk_ref, dv_ref, sems):
+def finish(fin_q, fin_k, fin_v, back_w, places_w, dq_hbm, dk_hbm, dv_hbm, rk, rv, dq_ref, dk_ref, dv_ref, sems):
     left = iota((1, 128), 1) < 64
-    copies = []
+    rk[...] = jnp.zeros_like(rk)
+    rv[...] = jnp.zeros_like(rv)
     for p in range(HEADS // 2):
         cols = pl.ds(p * 128, 128)
-        kvs, qs, rest = [], [], []
-        for a in range(2):
-            h = 2 * p + a
-            rows = back[h]
-            kvs.append(acc_kv[h] + nn(where_back[h, 0], rows))
-            qs.append(acc_q[h] + nn(where_back[h, 1], rows))
-            rest.append(nn(where_back[h, 2], rows))
-        dq = jnp.where(left, qs[0] + swap(rest[0]), swap(qs[1]) + rest[1])
-        dq_ref[:, cols] = (SCALE * dq).astype(BF)
-        dk_ref[:, cols] = (SCALE * jnp.where(left, kvs[0], swap(kvs[1]))).astype(BF)
-        dv_ref[:, cols] = jnp.where(left, swap(kvs[0]), kvs[1]).astype(BF)
-        if p % 2 == 1:
-            wide = pl.ds((p - 1) * 128, 256)
-            for i, (src, dst) in enumerate([(dq_ref, dq_hbm), (dk_ref, dk_hbm), (dv_ref, dv_hbm)]):
-                copies.append(pltpu.make_async_copy(src.at[:, wide], dst.at[:, wide], sems.at[i, p // 2]))
-                copies[-1].start()
+        a, b = back_w[2 * p].astype(F32), back_w[2 * p + 1].astype(F32)
+        rk[32 * p : 32 * p + 16, cols] = jnp.where(left, a, 0.0).astype(BF)
+        rk[32 * p + 16 : 32 * p + 32, cols] = jnp.where(left, 0.0, swap(b)).astype(BF)
+        rv[32 * p : 32 * p + 16, cols] = jnp.where(left, swap(a), 0.0).astype(BF)
+        rv[32 * p + 16 : 32 * p + 32, cols] = jnp.where(left, 0.0, b).astype(BF)
+    copies = []
+    for g in range(3):
+        cols = pl.ds(256 * g, 256)
+        kq = nn(places_w[...], rk[:, cols])
+        dk_ref[:, cols] = (SCALE * (fin_k[:, cols] + kq[:T])).astype(BF)
+        dq_ref[:, cols] = (SCALE * (fin_q[:, cols] + kq[T:])).astype(BF)
+        dv_ref[:, cols] = (fin_v[:, cols] + nn(places_w[0:T, :], rv[:, cols])).astype(BF)
+        for i, (src, dst) in enumerate([(dq_ref, dq_hbm), (dk_ref, dk_hbm), (dv_ref, dv_hbm)]):
+            copies.append(pltpu.make_async_copy(src.at[:, cols], dst.at[:, cols], sems.at[i, g]))
+            copies[-1].start()
     for copy in copies:
         copy.wait()
 
@@ -494,13 +523,14 @@
     parts = pl.pallas_call(
         kernel,
         out_shape=(
-            jax.ShapeDtypeStruct((HEADS, T, 128), F32),
-            jax.ShapeDtypeStruct((HEADS, T, 128), F32),
-            jax.ShapeDtypeStruct((HEADS, BACK, 128), BF),
-            jax.ShapeDtypeStruct((HEADS, 3, T, BACK), BF),
+            jax.ShapeDtypeStruct((T, HEADS * 64), F32),
+            jax.ShapeDtypeStruct((T, HEADS * 64), F32),
+            jax.ShapeDtypeStruct((T, HEADS * 64), F32),
+            jax.ShapeDtypeStruct((HEADS, 16, 128), BF),
+            jax.ShapeDtypeStruct((2 * T, HEADS * 16), BF),
         ),
         in_specs=[hbm] * 7,
-        out_specs=(vmem,) * 4,
+        out_specs=(vmem,) * 5,
         scratch_shapes=[
             pltpu.SMEM((HEADS,), I32),
             pltpu.SMEM((HEADS,), I32),
@@ -509,6 +539,11 @@
             v((T, HEADS * 64), BF),
             v((T, HEADS * 64), BF),
             v((T, HEADS * 64), BF),
+            v((HEADS, T, 128), F32),
+            v((HEADS, T, 128), F32),
+            v((HEADS, BACK, 128), BF),
+            v((HEADS, T, 64), BF),
+            v((HEADS, 2, T, 32), BF),
             v((HEADS, T, 128), BF),
             v((HEADS, T, 128), BF),
             v((HEADS, 16, 128), BF),
@@ -541,6 +576,8 @@
             v((N, 64, 128), BF),
             v((N, 64, 128), BF),
             v((N, 64, 128), BF),
+            v((8, 128), F32),
+            v((64, 128), BF),
             v((N, 96, 128), BF),
             v((N, 16, 128), BF),
             dma((7,)),
@@ -556,7 +593,7 @@
             dma, dma,
         ],
         compiler_params=pltpu.CompilerParams(
-            collective_id=0, has_side_effects=True, vmem_limit_bytes=44 * 1024 * 1024
+            collective_id=0, has_side_effects=True, vmem_limit_bytes=48 * 1024 * 1024
         ),
     )(
         *[
@@ -567,9 +604,9 @@
     return pl.pallas_call(
         finish,
         out_shape=(rows, rows, rows),
-        in_specs=[vmem] * 4,
+        in_specs=[vmem] * 5,
         out_specs=(hbm,) * 3,
-        scratch_shapes=[v((T, HEADS * 64), BF)] * 3 + [dma((3, 3))],
+        scratch_shapes=[v((HEADS * 16, HEADS * 64), BF)] * 2 + [v((T, HEADS * 64), BF)] * 3 + [dma((3, 3))],
         compiler_params=pltpu.CompilerParams(vmem_limit_bytes=40 * 1024 * 1024),
     )(*parts)
 

time: 47.9 us -> 46.1 us (0.962)
  Pallas kernels: 47.2 us -> 45.2 us
    pallas_call x2, Pallas kernels: 47.2 us -> 45.2 us  [the longest x1 43.8 us: per_device(): pl.pallas_call(kernel, out_shape=(jax.ShapeDtypeStruct((T, HEADS * 64), F...]
where the time goes in v5:
time: 46.1 us; the launch traced here: 46 us
  Pallas kernels  45.2 us (98%)
  between operations  0.8 us (2%)
    pallas_call x1, Pallas kernels, per_device(): pl.pallas_call(kernel, out_shape=(jax.ShapeDtypeStruct((T, HEADS * 64), F...  43.8 us
    pallas_call x1, Pallas kernels, per_device(): pl.pallas_call(finish, out_shape=(rows, rows, rows), in_specs=[vmem] * 5,...  1.43 us

profile of v5, /device:TPU:1, one launch (start us, length us, event | category | flops | bytes accessed | tf_op | source)
XLA Modules:
  0.0 46.0 jit_solution(3280150042708652493)
XLA Ops:
  0.6 43.8 %shard_map.94 = (f32[256,768]{1,0:T(8,128)S(1)}, f32[256,768]{1,0:T(8,128)S(1)}, f32[256,768]{1,0:T(8,128)S(1)}, bf16[12,16,128]{2,1,0:T(8,128)(2,1)S(1)}, bf16[512,192]{1,0:T(8,128)(2,1)S(1)}) custom-call(s32[12]{0:T(128)} %om_hbm.1, s32[12]{0:T(128)} %ow_hbm.1, bf16[256,768]{1,0:T(8,128)(2,1)} %q_hbm.1, bf16[256,768]{1,0:T(8,128)(2,1)} %k_hbm.1, ...), custom_call_target="tpu_custom_call" | custom-call | tf_op jit(solution)/shard_map/pallas_call | solution.py:523
  44.4 1.4 %shard_map.95 = (bf16[256,768]{1,0:T(8,128)(2,1)}, bf16[256,768]{1,0:T(8,128)(2,1)}, bf16[256,768]{1,0:T(8,128)(2,1)}) custom-call(f32[256,768]{1,0:T(8,128)S(1)} %get-tuple-element.8.fin_q, f32[256,768]{1,0:T(8,128)S(1)} %get-tuple-element.9.fin_k, f32[256,768]{1,0:T(8,128)S(1)} %get-tuple-element.10.fin_v, ...), custom_call_target="tpu_custom_call" | custom-call | tf_op jit(solution)/shard_map/pallas_call | solution.py:604

commit v6 on v5

--- a/solution.py
+++ b/solution.py
@@ -228,7 +228,7 @@
         gl[h] = (e * (d - dl[pl.ds(h, 1), :])).astype(BF)
         return 0
 
-    lax.fori_loop(0, HEADS, local_a, 0, unroll=3)
+    lax.fori_loop(0, HEADS, local_a, 0, unroll=6)
     @pl.when(active)
     def _():
         got_inner(rx_w.at[pl.ds(0, N - 1)], mw_r)
@@ -266,7 +266,7 @@
         where_kv[h] = onehot(iota((T, 64), 0) == 4 * iota((1, 64), 1) + om_ref[h])
         return 0
 
-    lax.fori_loop(0, HEADS, local_q, 0, unroll=3)
+    lax.fori_loop(0, HEADS, local_q, 0, unroll=6)
 
     @pl.when(active)
     def _():
@@ -312,7 +312,17 @@
 
         lane8, chunk8 = iota((8, 128), 1), iota((8, 128), 0)
 
-        def wide():
+        def share_lse():
+            lse_m = mm[...] + jnp.log(sm[...])
+            for j in range(8):
+                ls_tx[j] = jnp.where(
+                    chunk8 == 0, lse_m[j : j + 1], jnp.where(chunk8 == 1, lw[...], mm[j : j + 1, :])
+                )
+            for t in peers():
+                to_inner(ls_tx.at[t // 2], ls_rx.at[head], ls_s, ls_r, t).start()
+            ls_rx[head] = ls_tx[inner // 2]
+
+        def wide(last):
             got_inner(st_rx.at[pl.ds(0, N - 1)], st_r)
             ones = onehot(iota((8, N), 0) == (iota((8, N), 1) >> 1))
             rows = st_rx[:, 0, :]
@@ -328,6 +338,10 @@
             top_w = jnp.max(s, axis=0, keepdims=True)
             e = jnp.exp(s - top_w)
             lse_w = top_w + jnp.log(jnp.sum(e, axis=0, keepdims=True))
+            zeros64 = jnp.zeros((1, 64), F32)
+            lw[...] = jnp.broadcast_to(jnp.concatenate([lse_w, zeros64], axis=1), (8, 128))
+            if last:
+                share_lse()
             d = nt(all_y * half_v, x_w)
             ew = e.astype(BF)
             gw = (e * (d - dm[8:9, 0:64])).astype(BF)
@@ -336,7 +350,6 @@
             spot_row = jnp.full((1, 64), spot, I32)
             total_w = lse3(lse_w, lse_local_w[:, :64], jnp.where(spot_row >= 0, m_at_w, NEG))
             weight_w = jnp.exp(top_w - total_w)
-            zeros64 = jnp.zeros((1, 64), F32)
             col_w = jnp.broadcast_to(jnp.concatenate([weight_w, zeros64], axis=1), (128, 128)).T[0:64, 0:1]
             scaled = (x_w.astype(F32) * col_w).astype(BF)
             wp[...] = jnp.where(left, nn(gw, scaled), nn(ew, scaled)).astype(BF).reshape(N, 64, 128)
@@ -348,8 +361,7 @@
 
             dqw[...] = (tn(gw, all_y) * col_w).astype(BF)
 
-            lse_w = jnp.concatenate([lse_w, zeros64], axis=1)
-            lw[...] = jnp.broadcast_to(lse_w, (8, 128))
+            lse_w = lw[0:1, :]
             n128 = iota((128, 128), 1)
             spread = onehot(((n128 & 7) == (iota((128, 128), 0) >> 4)) & (n128 < 64))
             w_at_m = sum3(nt(split3(jnp.where((lane8 >> 3) == chunk8, lse_w, 0.0)), spread))
@@ -358,22 +370,18 @@
         late = outer >= 8
         for u in range(4):
             if u == 3:
-                pl.when(late)(wide)
+                pl.when(late)(lambda: wide(False))
             mid_a(u)
-        pl.when(jnp.logical_not(late))(wide)
+        pl.when(late)(share_lse)
+        pl.when(jnp.logical_not(late))(lambda: wide(True))
 
         lse_m = mm[...] + jnp.log(sm[...])
         weight_m = jnp.exp(mm[...] - lse3(lse_m, lm[...], wm[...]))
         columns = jnp.concatenate([weight_m, jnp.zeros((120, 128), F32)], axis=0).T
         for j in range(8):
-            ls_tx[j] = jnp.where(chunk8 == 0, lse_m[j : j + 1], jnp.where(chunk8 == 1, lw[...], mm[j : j + 1, :]))
             col = columns[:, j : j + 1]
             x = rx[2 * j : 2 * j + 2, 64:128, :].reshape(128, 128).astype(F32)
             xw_all[j // 2, 128 * (j % 2) : 128 * (j % 2) + 128, :] = (x * col).astype(BF)
-        for t in peers():
-            to_inner(ls_tx.at[t // 2], ls_rx.at[head], ls_s, ls_r, t).start()
-        ls_rx[head] = ls_tx[inner // 2]
-
         def mid_b(u, _):
             kb = block_of(u)
             from_g = jnp.zeros((T, 128), F32)

time: 46.1 us -> 45.5 us (0.987)
  Pallas kernels: 45.2 us -> 44.6 us
    pallas_call x1, Pallas kernels: 43.8 us -> 43.2 us  [per_device(): pl.pallas_call(kernel, out_shape=(jax.ShapeDtypeStruct((T, HEADS * 64), F...]
where the time goes in v6:
time: 45.5 us; the launch traced here: 45.4 us
  Pallas kernels  44.6 us (98%)
  between operations  0.8 us (2%)
    pallas_call x1, Pallas kernels, per_device(): pl.pallas_call(kernel, out_shape=(jax.ShapeDtypeStruct((T, HEADS * 64), F...  43.2 us
    pallas_call x1, Pallas kernels, per_device(): pl.pallas_call(finish, out_shape=(rows, rows, rows), in_specs=[vmem] * 5,...  1.43 us

profile of v6, /device:TPU:1, one launch (start us, length us, event | category | flops | bytes accessed | tf_op | source)
XLA Modules:
  0.0 45.4 jit_solution(1453419763503515735)
XLA Ops:
  0.6 43.2 %shard_map.94 = (f32[256,768]{1,0:T(8,128)S(1)}, f32[256,768]{1,0:T(8,128)S(1)}, f32[256,768]{1,0:T(8,128)S(1)}, bf16[12,16,128]{2,1,0:T(8,128)(2,1)S(1)}, bf16[512,192]{1,0:T(8,128)(2,1)S(1)}) custom-call(s32[12]{0:T(128)} %om_hbm.1, s32[12]{0:T(128)} %ow_hbm.1, bf16[256,768]{1,0:T(8,128)(2,1)} %q_hbm.1, bf16[256,768]{1,0:T(8,128)(2,1)} %k_hbm.1, ...), custom_call_target="tpu_custom_call" | custom-call | tf_op jit(solution)/shard_map/pallas_call | solution.py:531
  43.8 1.4 %shard_map.95 = (bf16[256,768]{1,0:T(8,128)(2,1)}, bf16[256,768]{1,0:T(8,128)(2,1)}, bf16[256,768]{1,0:T(8,128)(2,1)}) custom-call(f32[256,768]{1,0:T(8,128)S(1)} %get-tuple-element.8.fin_q, f32[256,768]{1,0:T(8,128)S(1)} %get-tuple-element.9.fin_k, f32[256,768]{1,0:T(8,128)S(1)} %get-tuple-element.10.fin_v, ...), custom_call_target="tpu_custom_call" | custom-call | tf_op jit(solution)/shard_map/pallas_call | solution.py:612
